TPU v7x, 512 devices: a whole 4x4x16 slice. The times are simulated.
512 devices in a mesh: group: 16 (over z_lo, y), resp: 32 (over z_hi, x, core).
Axes of the slice: x: 4, y: 4, z: 16 (z_hi: 4, z_lo: 4; z = z_hi * 4 + z_lo), core: 2. Of those that a mesh axis runs over, the one named last changes fastest.
Arguments:
- queries: bfloat16 [16, 32, 128, 2048], P('group', 'resp'), may hold values from -6 to 6
- response_keys: bfloat16 [16, 32, 128, 512], P('group', 'resp'), may hold values from -6 to 6
- response_values: bfloat16 [16, 32, 128, 512], P('group', 'resp'), may hold values from -6 to 6
- prompt_key_rows: bfloat16 [16, 512, 512], P('group', 'resp'), may hold values from -6 to 6
- prompt_value_rows: bfloat16 [16, 512, 512], P('group', 'resp'), may hold values from -6 to 6
- upstream: bfloat16 [16, 32, 128, 2048], P('group', 'resp'), may hold values from -6 to 6
- rewards: float32 [16, 32], P('group', 'resp'), may hold values from 0 to 1
- lengths: int32 [16, 32], P('group', 'resp'), may hold values from 16 to 128
Outputs:
- grad_queries: bfloat16 [16, 32, 128, 2048], P('group', 'resp')
- grad_own_keys: bfloat16 [16, 32, 128, 512], P('group', 'resp')
- grad_own_values: bfloat16 [16, 32, 128, 512], P('group', 'resp')
- grad_prompt_keys: float32 [16, 512, 512], P('group', 'resp')
- grad_prompt_values: float32 [16, 512, 512], P('group', 'resp')
All inputs are finite; a program needn't handle non-finite values.
Results may differ from a plain program's by a relative error of at most 0.012.
The roundings to bfloat16 on the way count: a program that leaves them out, or rounds other values in their place, can miss the bound.
Values may be sent and summed in bfloat16 or wider, within the bound.
A program may use at most 64 MiB of HBM per device.

v0:
```python
import jax
import jax.numpy as jnp
from jax import lax
from jax.sharding import PartitionSpec as P

QUERY_HEADS = 16
KEY_HEADS = 4
HEAD_SIZE = 128


def on_device(
    queries,
    response_keys,
    response_values,
    prompt_key_rows,
    prompt_value_rows,
    upstream,
    rewards,
    lengths,
):
    score_scale = HEAD_SIZE ** (-0.5)
    group_slice = QUERY_HEADS // KEY_HEADS
    row_count = queries.shape[2]
    query_matrix = queries[0, 0]
    key_rows = response_keys[0, 0]
    value_rows = response_values[0, 0]
    reward = rewards[0, 0]
    live_count = lengths[0, 0].astype(jnp.float32)
    reward_total = lax.psum(reward, "resp")
    total = lax.psum(live_count, ("group", "resp"))
    advantage = reward - reward_total / lax.axis_size("resp")
    steps = jnp.arange(row_count)
    live = (steps < lengths[0, 0]).astype(jnp.float32)
    coef = advantage * live / total
    output_gradient = (upstream[0, 0].astype(jnp.float32) * coef[:, None]).astype(jnp.bfloat16)
    causal = steps[None, :] <= steps[:, None]
    query_four_axes = query_matrix.reshape(row_count, KEY_HEADS, group_slice, HEAD_SIZE)
    prompt_len = prompt_key_rows.shape[1] * lax.axis_size("resp")
    prompt_k, prompt_v = (
        lax.all_gather(prompt_key_rows[0], "resp", axis=0, tiled=True),
        lax.all_gather(prompt_value_rows[0], "resp", axis=0, tiled=True),
    )
    allowed = jnp.concatenate([jnp.ones((row_count, prompt_len), jnp.bool_), causal], axis=1)
    query_pieces = []
    key_pieces = []
    value_pieces = []
    for head_number in range(KEY_HEADS):
        lower = head_number * HEAD_SIZE
        prompt_head_keys = prompt_k[:, lower : lower + HEAD_SIZE]
        prompt_head_values = prompt_v[:, lower : lower + HEAD_SIZE]
        keys_head = jnp.concatenate(
            [prompt_head_keys, key_rows[:, lower : lower + HEAD_SIZE]], axis=0
        )
        values_head = jnp.concatenate(
            [prompt_head_values, value_rows[:, lower : lower + HEAD_SIZE]], axis=0
        )
        query_head = query_four_axes[:, head_number]
        grad_head = output_gradient[
            :, head_number * group_slice * HEAD_SIZE : (head_number + 1) * group_slice * HEAD_SIZE
        ].reshape(row_count, group_slice, HEAD_SIZE)
        scores = (
            jnp.einsum("tqd,kd->qtk", query_head, keys_head, preferred_element_type=jnp.float32)
            * score_scale
        )
        scores = jnp.where(allowed, scores, -1e30)
        top_row = jnp.max(scores, axis=-1)
        lse = top_row + jnp.log(jnp.sum(jnp.exp(scores - top_row[..., None]), axis=-1))
        probs = jnp.exp(scores - lse[..., None])
        probability_narrow = probs.astype(jnp.bfloat16)
        out = jnp.einsum(
            "qtk,kd->tqd", probability_narrow, values_head, preferred_element_type=jnp.float32
        )
        delta = jnp.sum(grad_head.astype(jnp.float32) * out, axis=-1).T
        grad_probs = jnp.einsum(
            "tqd,kd->qtk", grad_head, values_head, preferred_element_type=jnp.float32
        )
        score_gradient = (probs * (grad_probs - delta[..., None])).astype(jnp.bfloat16)
        grad_query = score_scale * jnp.einsum(
            "qtk,kd->tqd", score_gradient, keys_head, preferred_element_type=jnp.float32
        )
        query_pieces.append(
            grad_query.reshape(row_count, group_slice * HEAD_SIZE).astype(jnp.bfloat16)
        )
        key_piece = score_scale * jnp.einsum(
            "qtk,tqd->kd", score_gradient, query_head, preferred_element_type=jnp.float32
        )
        value_piece = jnp.einsum(
            "qtk,tqd->kd", probability_narrow, grad_head, preferred_element_type=jnp.float32
        )
        key_pieces.append(key_piece)
        value_pieces.append(value_piece)
    grad_query_all = jnp.concatenate(query_pieces, axis=1)
    grad_key_all = jnp.concatenate(key_pieces, axis=1)
    grad_value_all = jnp.concatenate(value_pieces, axis=1)
    prompt_dk, prompt_dv = (
        lax.psum_scatter(grad_key_all[:prompt_len], "resp", scatter_dimension=0, tiled=True),
        lax.psum_scatter(grad_value_all[:prompt_len], "resp", scatter_dimension=0, tiled=True),
    )
    return (
        grad_query_all[None, None],
        grad_key_all[prompt_len:].astype(jnp.bfloat16)[None, None],
        grad_value_all[prompt_len:].astype(jnp.bfloat16)[None, None],
        prompt_dk[None],
        prompt_dv[None],
    )


def solution(mesh):
    placed = (
        P("group", "resp", None, None),
        P("group", "resp", None, None),
        P("group", "resp", None, None),
        P("group", "resp", None),
        P("group", "resp", None),
        P("group", "resp", None, None),
        P("group", "resp"),
        P("group", "resp"),
    )
    return jax.shard_map(
        on_device,
        mesh=mesh,
        in_specs=placed,
        out_specs=(
            P("group", "resp", None, None),
            P("group", "resp", None, None),
            P("group", "resp", None, None),
            P("group", "resp", None),
            P("group", "resp", None),
        ),
        check_vma=False,
    )
```

profile of v0, /device:TPU:1, one launch (start us, length us, event | category | flops | bytes accessed | tf_op | source)
XLA Modules:
  0.0 552.6 jit_solution(5206463712560285044)
XLA Ops:
  7.9 111.0 %psum.15 = f32[]{:T(128)} all-reduce(f32[]{:T(128)S(6)} %convert_element_type.89), channel_id=1, replica_groups=mesh['group'=16,'resp'=32] {'group','resp'}, use_global_device_ids=true, to_apply=%region_3.4 | all-reduce | flops 1 | bytes 8 | tf_op jit(solution)/shard_map/psum | solution.py:30
  119.5 85.1 %psum.14 = f32[]{:T(128)} all-reduce(f32[]{:T(128)} %bitcast.12), channel_id=1, replica_groups=mesh['group'=16,'resp'=32] {'resp'}, use_global_device_ids=true, to_apply=%region_2.3 | all-reduce | flops 1 | bytes 8 | tf_op jit(solution)/shard_map/psum | solution.py:29
  204.7 1.4 fusion.72
  206.1 1.5 fusion.71
  207.6 1.3 copy.103
  208.9 52.6 %all-gather = bf16[1,512,512]{2,1,0:T(8,128)(2,1)S(1)} all-gather(bf16[1,16,512]{2,1,0:T(8,128)(2,1)S(1)} %copy-done.40), channel_id=2, replica_groups=mesh['group'=16,'resp'=32] {'resp'}, dimensions={1}, use_global_device_ids=true | all-gather | bytes 540672 | tf_op jit(solution)/shard_map/all_gather | solution.py:40
  262.3 48.9 %all-gather.1 = bf16[1,512,512]{2,1,0:T(8,128)(2,1)S(1)} all-gather(bf16[1,16,512]{2,1,0:T(8,128)(2,1)S(1)} %copy-done.41), channel_id=3, replica_groups=mesh['group'=16,'resp'=32] {'resp'}, dimensions={1}, use_global_device_ids=true | all-gather | bytes 540672 | tf_op jit(solution)/shard_map/all_gather | solution.py:41
  315.6 1.3 fusion.73
  323.5 0.8 copy-done.8
  324.8 1.1 copy-done.10
  325.9 1.1 slice.140
  327.0 2.5 copy.189
  329.6 1.3 convolution_bitcast_fusion.7
  331.3 0.9 copy-done.1
  332.6 0.9 copy-done.3
  334.0 1.0 copy-done.11
  335.2 1.3 copy.191
  339.0 1.0 fusion.50
  340.7 1.0 fusion.49
  342.5 0.8 maximum_bitcast_fusion
  343.3 88.1 %reduce-scatter.7.cloned.1.call-done = f32[16,512]{1,0:T(8,128)} async-done(((f32[512,512]{1,0:T(8,128)}), f32[16,512]{1,0:T(8,128)}) %reduce-scatter.7.cloned.1.call-update) | async-done | bytes 32784
  431.5 0.9 copy.190
  433.1 111.1 %reduce-scatter.9.cloned.1.call-done = f32[16,512]{1,0:T(8,128)} async-done(((f32[512,512]{1,0:T(8,128)}), f32[16,512]{1,0:T(8,128)}) %reduce-scatter.9.cloned.1.call-update) | async-done | bytes 32784
  544.2 0.9 copy.192
  (132 shorter events, 18.0 us)
Async XLA Ops:
  7.2 201.7 %copy-start.40 = (bf16[1,16,512]{2,1,0:T(8,128)(2,1)S(1)}, bf16[1,16,512]{2,1,0:T(8,128)(2,1)}, u32[]{:S(2)}) copy-start(bf16[1,16,512]{2,1,0:T(8,128)(2,1)} %param.11) | copy-start | bytes 49156
  7.2 424.3 %reduce-scatter.7.cloned.1.call-start = ((), (), s32[]{:S(2)}) async-start(), calls=%async_computation.2 | async-start | bytes 1081344
  206.1 107.7 %copy-start.38 = (bf16[128,128]{1,0:T(8,128)(2,1)}, bf16[128,128]{1,0:T(8,128)(2,1)S(1)}, u32[]{:S(2)}) copy-start(bf16[128,128]{1,0:T(8,128)(2,1)S(1)} %get-tuple-element.36) | copy-start | bytes 98308
  207.6 54.7 %copy-start.41 = (bf16[1,16,512]{2,1,0:T(8,128)(2,1)S(1)}, bf16[1,16,512]{2,1,0:T(8,128)(2,1)}, u32[]{:S(2)}) copy-start(bf16[1,16,512]{2,1,0:T(8,128)(2,1)} %param.12) | copy-start | bytes 49156
  208.9 106.2 %copy-start.12 = (bf16[1,1,128,2048]{2,3,1,0:T(8,128)(2,1)}, bf16[1,1,128,2048]{2,3,1,0:T(8,128)(2,1)S(1)}, u32[]{:S(2)}) copy-start(bf16[1,1,128,2048]{2,3,1,0:T(8,128)(2,1)S(1)} %copy.103) | copy-start | bytes 1572868
  261.5 50.4 %copy-start.20 = (bf16[1,1,128,2048]{3,2,1,0:T(8,128)(2,1)S(1)}, bf16[1,1,128,2048]{3,2,1,0:T(8,128)(2,1)}, u32[]{:S(2)}) copy-start(bf16[1,1,128,2048]{3,2,1,0:T(8,128)(2,1)} %param.13) | copy-start | bytes 1572868
  262.3 51.5 %copy-start.27 = (bf16[512,128]{1,0:T(8,128)(2,1)}, bf16[512,128]{1,0:T(8,128)(2,1)S(1)}, u32[]{:S(2)}) copy-start(bf16[512,128]{1,0:T(8,128)(2,1)S(1)} %get-tuple-element.24) | copy-start | bytes 393220
  313.7 3.8 copy-start.14
  315.6 1.5 copy-start.19
  315.6 1.5 copy-start.31
  317.5 1.9 copy-start.23
  317.6 1.9 copy-start.34
  329.5 214.6 %reduce-scatter.9.cloned.1.call-start = ((), (), s32[]{:S(2)}) async-start(), calls=%async_computation.3 | async-start | bytes 1081344
  329.6 1.3 copy-start.15
  330.9 1.3 copy-start.1
  332.2 1.3 copy-start.3
  335.2 1.4 copy-start.28
  335.2 1.4 copy-start.39
  336.6 1.5 copy-start.7
  336.6 1.5 copy-start.24
  336.6 1.5 copy-start.35
  336.9 1.6 copy-start.9
  336.9 1.6 copy-start.22
  337.0 1.6 copy-start.33
  (20 other events, 19.4 us)
Sparse Core Ops, SparseCore 0:
  329.7 101.7 reduce-scatter.6
  436.4 107.6 reduce-scatter.8
where the time goes:
time: 555 us; the launch traced here: 553 us
  blocking collectives  298 us (54%)
  waiting for transfers between devices  199 us (36%)
  local copies, waits for them, and re-layouts  26.2 us (5%)
  between operations  16.7 us (3%)
  matrix products  10.1 us (2%)
    unnamed x4, waiting for transfers between devices  199 us
    psum x1, blocking collectives, on_device(): total = lax.psum(live_count, ('group', 'resp'))  111 us
    psum x1, blocking collectives, on_device(): reward_total = lax.psum(reward, 'resp')  85.1 us
    all_gather x1, blocking collectives, on_device(): lax.all_gather(prompt_key_rows[0], 'resp', axis=0, tiled=True)  52.6 us
    all_gather x1, blocking collectives, on_device(): lax.all_gather(prompt_value_rows[0], 'resp', axis=0, tiled=True)  48.9 us
    unnamed x94, local copies, waits for them, and re-layouts  18.1 us
  transfers between devices with their start and end apart: 2, of which 2 were waited for; matrix products, arithmetic and copies ran while one was open for 2% of the time, Pallas kernels for 0%

commit v1 on v0

v1 whole, which is shorter than its diff:
```python
import functools

import jax
import jax.numpy as jnp
from jax import lax
from jax.experimental import pallas as pl
from jax.experimental.pallas import tpu as pltpu
from jax.sharding import PartitionSpec as P

MESH = pl.DeviceIdType.MESH
KEY_HEADS = 4
QUERY_PER_KV = 4
HEAD = 128
TOKENS = 128
SCALE = HEAD ** (-0.5)
LOG2E = 1.4426950408889634
F32 = jnp.float32
BF16 = jnp.bfloat16


def dot(a, b, a_dim, b_dim):
    return lax.dot_general(
        a, b, (((a_dim,), (b_dim,)), ((), ())), preferred_element_type=F32
    )


def kernel(
    dims,
    q_hbm,
    ok_hbm,
    ov_hbm,
    pk_hbm,
    pv_hbm,
    up_hbm,
    reward_ref,
    length_ref,
    gq_hbm,
    gok_hbm,
    gov_hbm,
    gpk_hbm,
    gpv_hbm,
    q_v,
    up_v,
    own_v,
    kv,
    stat,
    stat_y,
    stat_l,
    stat_z,
    stat_x,
    stat_c,
    so_ref,
    s_ref,
    p_ref,
    dp_ref,
    pb_ref,
    ds_ref,
    acc,
    rc,
    xs,
    rx,
    zacc,
    zs,
    rz,
    gq_v,
    go_v,
    gp_v,
    in_sem,
    pin_sem,
    out_sem,
    gz_s,
    gz_r,
    gx_s,
    gx_r,
    gc_s,
    gc_r,
    sc_s,
    sc_r,
    sx_s,
    sx_r,
    sz_s,
    sz_r,
    ty_s,
    ty_r,
    tl_s,
    tl_r,
    tz_s,
    tz_r,
    tx_s,
    tx_r,
    tc_s,
    tc_r,
):
    nl, ny, nz, nx = dims
    prompt = nz * nx * 2 * 16
    rows = QUERY_PER_KV * TOKENS
    gi, ri = lax.axis_index("group"), lax.axis_index("resp")
    mc = lax.rem(ri, 2)
    mx = lax.rem(lax.div(ri, 2), nx)
    mz = lax.div(ri, 2 * nx)
    my = lax.rem(gi, ny)
    ml = lax.div(gi, ny)

    def device(c=mc, x=mx, z=mz, y=my, l=ml):
        return (l * ny + y, (z * nx + x) * 2 + c)

    def ahead(me, d, n):
        return lax.rem(me + d, n)

    def remote(src, dst, send, recv, to):
        return pltpu.make_async_remote_copy(
            src_ref=src,
            dst_ref=dst,
            send_sem=send,
            recv_sem=recv,
            device_id=to,
            device_id_type=MESH,
        )

    def head_cols(g):
        return slice(g * HEAD, (g + 1) * HEAD)

    shard_in = []
    for g in range(KEY_HEADS):
        pair = []
        for i, src in enumerate((pk_hbm, pv_hbm)):
            pair.append(
                pltpu.make_async_copy(
                    src.at[:, head_cols(g)],
                    kv.at[g, i, mc, mx, mz],
                    pin_sem.at[g, i],
                )
            )
            pair[-1].start()
        shard_in.append(pair)
    loads = [
        pltpu.make_async_copy(src, dst, in_sem.at[i])
        for i, (src, dst) in enumerate(
            (
                (q_hbm, q_v),
                (ok_hbm, own_v.at[0]),
                (ov_hbm, own_v.at[1]),
                (up_hbm, up_v),
            )
        )
    ]
    for load in loads:
        load.start()

    reward = reward_ref[0, 0]
    length = length_ref[0, 0]
    stat[0, 0:8] = jnp.full((8, 128), reward, F32)
    stat[0, 8:16] = jnp.full((8, 128), length.astype(F32), F32)

    partners = [device(c=1 - mc)]
    partners += [device(x=ahead(mx, d, nx)) for d in range(1, nx)]
    partners += [device(z=ahead(mz, d, nz)) for d in range(1, nz)]
    partners += [device(y=ahead(my, d, ny)) for d in range(1, ny)]
    partners += [device(l=ahead(ml, d, nl)) for d in range(1, nl)]
    barrier = pltpu.get_barrier_semaphore()
    for partner in partners:
        pl.semaphore_signal(barrier, inc=1, device_id=partner, device_id_type=MESH)
    pl.semaphore_wait(barrier, len(partners))

    sent = []

    def send(copies):
        for copy in copies:
            copy.start()
        sent.extend(copies)
        return copies

    def arrive(copies):
        for copy in copies:
            copy.wait_recv()

    def stat_send(step, into, s_sem, r_sem, name, me, n):
        return send(
            [
                remote(
                    stat.at[step],
                    into.at[d - 1],
                    s_sem.at[d - 1],
                    r_sem.at[d - 1],
                    device(**{name: ahead(me, d, n)}),
                )
                for d in range(1, n)
            ]
        )

    def stat_sum(step, copies, into, n, both):
        arrive(copies)
        block = stat[step]
        total = block[8:16]
        wins = block[0:8]
        for d in range(n - 1):
            total = total + into[d, 8:16]
            if both:
                wins = wins + into[d, 0:8]
        stat[step + 1, 0:8] = wins
        stat[step + 1, 8:16] = total

    def gather_z(g):
        mine = kv.at[g, :, mc, mx, mz]
        return send(
            [
                remote(
                    mine,
                    mine,
                    gz_s.at[g, d - 1],
                    gz_r.at[g, d - 1],
                    device(z=ahead(mz, d, nz)),
                )
                for d in range(1, nz)
            ]
        )

    def gather_x(g):
        mine = kv.at[g, :, mc, mx]
        return send(
            [
                remote(
                    mine,
                    mine,
                    gx_s.at[g, d - 1],
                    gx_r.at[g, d - 1],
                    device(x=ahead(mx, d, nx)),
                )
                for d in range(1, nx)
            ]
        )

    def gather_c(g):
        mine = kv.at[g, :, mc]
        return send(
            [remote(mine, mine, gc_s.at[g], gc_r.at[g], device(c=1 - mc))]
        )

    def reduce_c(g):
        return send(
            [
                remote(
                    acc.at[g, :, 1 - mc],
                    rc.at[g],
                    sc_s.at[g],
                    sc_r.at[g],
                    device(c=1 - mc),
                )
            ]
        )

    def reduce_x(g, copies):
        arrive(copies)
        xs[g] = (acc[g, :, mc] + rc[g]).astype(BF16)
        return send(
            [
                remote(
                    xs.at[g, :, ahead(mx, d, nx)],
                    rx.at[g, d - 1],
                    sx_s.at[g, d - 1],
                    sx_r.at[g, d - 1],
                    device(x=ahead(mx, d, nx)),
                )
                for d in range(1, nx)
            ]
        )

    def reduce_z(g, copies):
        arrive(copies)
        part = acc[g, :, mc, mx] + rc[g, :, mx]
        for d in range(nx - 1):
            part = part + rx[g, d].astype(F32)
        zacc[g] = part
        zs[g] = part.astype(BF16)
        return send(
            [
                remote(
                    zs.at[g, :, ahead(mz, d, nz)],
                    rz.at[g, d - 1],
                    sz_s.at[g, d - 1],
                    sz_r.at[g, d - 1],
                    device(z=ahead(mz, d, nz)),
                )
                for d in range(1, nz)
            ]
        )

    def reduce_end(g, copies):
        arrive(copies)
        part = zacc[g, :, mz]
        for d in range(nz - 1):
            part = part + rz[g, d].astype(F32)
        gp_v[0, :, head_cols(g)] = part[0]
        gp_v[1, :, head_cols(g)] = part[1]

    def query_cols(g, j):
        lower = (g * QUERY_PER_KV + j) * HEAD
        return slice(lower, lower + HEAD)

    def queries_of(g):
        return jnp.concatenate(
            [q_v[:, query_cols(g, j)] for j in range(QUERY_PER_KV)], axis=0
        )

    def own_scores(g):
        key = lax.broadcasted_iota(jnp.int32, (TOKENS, rows), 0)
        step = lax.broadcasted_iota(jnp.int32, (TOKENS, rows), 1) & (TOKENS - 1)
        scores = dot(own_v[0, :, head_cols(g)], queries_of(g), 1, 1)
        so_ref[g] = jnp.where(key <= step, scores, -1e30)

    def forward(g):
        s_ref[...] = dot(kv[g, 0].reshape(prompt, HEAD), queries_of(g), 1, 1)
        top = jnp.maximum(
            jnp.max(s_ref[...], axis=0, keepdims=True),
            jnp.max(so_ref[g], axis=0, keepdims=True),
        )
        p_ref[0:prompt] = jnp.exp2((s_ref[...] - top) * (SCALE * LOG2E))
        p_ref[prompt:] = jnp.exp2((so_ref[g] - top) * (SCALE * LOG2E))
        inverse = 1.0 / jnp.sum(p_ref[...], axis=0, keepdims=True)
        probs = p_ref[...] * inverse
        p_ref[...] = probs
        pb_ref[...] = probs.astype(BF16)

    def backward(g, coef):
        q_g = queries_of(g)
        keys = kv[g, 0].reshape(prompt, HEAD)
        own_keys = own_v[0, :, head_cols(g)]
        grad_out = jnp.concatenate(
            [
                (up_v[:, query_cols(g, j)].astype(F32) * coef).astype(BF16)
                for j in range(QUERY_PER_KV)
            ],
            axis=0,
        )
        dp_ref[0:prompt] = dot(kv[g, 1].reshape(prompt, HEAD), grad_out, 1, 1)
        dp_ref[prompt:] = dot(own_v[1, :, head_cols(g)], grad_out, 1, 1)
        grad_values = dot(pb_ref[...], grad_out, 1, 0)
        acc[g, 1] = grad_values[0:prompt].reshape(2, nx, nz, 16, HEAD)
        go_v[1, :, head_cols(g)] = grad_values[prompt:].astype(BF16)
        delta = jnp.sum(pb_ref[...].astype(F32) * dp_ref[...], axis=0, keepdims=True)
        ds_ref[...] = (p_ref[...] * (dp_ref[...] - delta)).astype(BF16)
        grad_keys = SCALE * dot(ds_ref[...], q_g, 1, 0)
        acc[g, 0] = grad_keys[0:prompt].reshape(2, nx, nz, 16, HEAD)
        go_v[0, :, head_cols(g)] = grad_keys[prompt:].astype(BF16)

    def query_gradient(g):
        keys = kv[g, 0].reshape(prompt, HEAD)
        own_keys = own_v[0, :, head_cols(g)]
        turned = SCALE * (
            dot(keys, ds_ref[0:prompt], 0, 0) + dot(own_keys, ds_ref[prompt:], 0, 0)
        )
        for j in range(QUERY_PER_KV):
            block = turned[:, j * TOKENS : (j + 1) * TOKENS]
            gq_v[:, query_cols(g, j)] = block.T.astype(BF16)

    t_y = stat_send(0, stat_y, ty_s, ty_r, "y", my, ny)
    on_z, on_x, on_c = [], [], []
    for g in range(KEY_HEADS):
        for copy in shard_in[g]:
            copy.wait()
        on_z.append(gather_z(g))
    for load in loads[0:3]:
        load.wait()
    for g in range(KEY_HEADS):
        own_scores(g)
    stat_sum(0, t_y, stat_y, ny, False)
    t_l = stat_send(1, stat_l, tl_s, tl_r, "l", ml, nl)
    arrive(on_z[0])
    on_x.append(gather_x(0))
    stat_sum(1, t_l, stat_l, nl, False)
    t_z = stat_send(2, stat_z, tz_s, tz_r, "z", mz, nz)
    arrive(on_z[1])
    on_x.append(gather_x(1))
    arrive(on_x[0])
    on_c.append(gather_c(0))
    stat_sum(2, t_z, stat_z, nz, True)
    t_x = stat_send(3, stat_x, tx_s, tx_r, "x", mx, nx)
    arrive(on_z[2])
    on_x.append(gather_x(2))
    arrive(on_x[1])
    on_c.append(gather_c(1))
    stat_sum(3, t_x, stat_x, nx, True)
    t_c = stat_send(4, stat_c, tc_s, tc_r, "c", mc, 2)
    arrive(on_z[3])
    on_x.append(gather_x(3))
    arrive(on_c[0])
    forward(0)
    arrive(on_x[2])
    on_c.append(gather_c(2))
    stat_sum(4, t_c, stat_c, 2, True)

    advantage = reward - stat[5, 0:1] / (nz * nx * 2)
    weight = jnp.broadcast_to(advantage / stat[5, 8:9], (TOKENS, HEAD))
    step = lax.broadcasted_iota(jnp.int32, (TOKENS, HEAD), 0)
    coef = jnp.where(step < length, weight, 0.0)
    loads[3].wait()

    backward(0, coef)
    off_c = [reduce_c(0)]
    arrive(on_x[3])
    on_c.append(gather_c(3))
    query_gradient(0)
    arrive(on_c[1])
    forward(1)
    off_x = [reduce_x(0, off_c[0])]
    backward(1, coef)
    off_c.append(reduce_c(1))
    query_gradient(1)
    off_z = [reduce_z(0, off_x[0])]
    arrive(on_c[2])
    forward(2)
    off_x.append(reduce_x(1, off_c[1]))
    backward(2, coef)
    off_c.append(reduce_c(2))
    query_gradient(2)
    off_z.append(reduce_z(1, off_x[1]))
    arrive(on_c[3])
    forward(3)
    off_x.append(reduce_x(2, off_c[2]))
    backward(3, coef)
    off_c.append(reduce_c(3))
    stores = [
        pltpu.make_async_copy(src, dst, out_sem.at[i])
        for i, (src, dst) in enumerate(
            (
                (go_v.at[0], gok_hbm),
                (go_v.at[1], gov_hbm),
                (gq_v, gq_hbm),
                (gp_v.at[0], gpk_hbm),
                (gp_v.at[1], gpv_hbm),
            )
        )
    ]
    stores[0].start()
    stores[1].start()
    off_z.append(reduce_z(2, off_x[2]))
    off_x.append(reduce_x(3, off_c[3]))
    query_gradient(3)
    stores[2].start()
    reduce_end(0, off_z[0])
    reduce_end(1, off_z[1])
    off_z.append(reduce_z(3, off_x[3]))
    reduce_end(2, off_z[2])
    reduce_end(3, off_z[3])
    stores[3].start()
    stores[4].start()
    for copy in sent:
        copy.wait_send()
    for store in stores:
        store.wait()


def on_device(
    dims,
    queries,
    response_keys,
    response_values,
    prompt_key_rows,
    prompt_value_rows,
    upstream,
    rewards,
    lengths,
):
    nl, ny, nz, nx = dims
    kvh, rows = KEY_HEADS, QUERY_PER_KV * TOKENS
    prompt = nz * nx * 2 * 16
    joined = prompt + TOKENS
    wide, narrow = queries.shape[3], response_keys.shape[3]
    shard = prompt_key_rows.shape[1]
    vmem, sem = pltpu.VMEM, pltpu.SemaphoreType.DMA
    anywhere = pl.BlockSpec(memory_space=pl.ANY)
    scalar = pl.BlockSpec(memory_space=pltpu.SMEM)
    results = pl.pallas_call(
        functools.partial(kernel, dims),
        out_shape=(
            jax.ShapeDtypeStruct((TOKENS, wide), BF16),
            jax.ShapeDtypeStruct((TOKENS, narrow), BF16),
            jax.ShapeDtypeStruct((TOKENS, narrow), BF16),
            jax.ShapeDtypeStruct((shard, narrow), F32),
            jax.ShapeDtypeStruct((shard, narrow), F32),
        ),
        in_specs=[anywhere] * 6 + [scalar] * 2,
        out_specs=[anywhere] * 5,
        scratch_shapes=[
            vmem((TOKENS, wide), BF16),
            vmem((TOKENS, wide), BF16),
            vmem((2, TOKENS, narrow), BF16),
            vmem((kvh, 2, 2, nx, nz, 16, HEAD), BF16),
            vmem((6, 16, 128), F32),
            vmem((max(ny - 1, 1), 16, 128), F32),
            vmem((max(nl - 1, 1), 16, 128), F32),
            vmem((max(nz - 1, 1), 16, 128), F32),
            vmem((max(nx - 1, 1), 16, 128), F32),
            vmem((1, 16, 128), F32),
            vmem((kvh, TOKENS, rows), F32),
            vmem((prompt, rows), F32),
            vmem((joined, rows), F32),
            vmem((joined, rows), F32),
            vmem((joined, rows), BF16),
            vmem((joined, rows), BF16),
            vmem((kvh, 2, 2, nx, nz, 16, HEAD), F32),
            vmem((kvh, 2, nx, nz, 16, HEAD), F32),
            vmem((kvh, 2, nx, nz, 16, HEAD), BF16),
            vmem((kvh, nx - 1, 2, nz, 16, HEAD), BF16),
            vmem((kvh, 2, nz, 16, HEAD), F32),
            vmem((kvh, 2, nz, 16, HEAD), BF16),
            vmem((kvh, nz - 1, 2, 16, HEAD), BF16),
            vmem((TOKENS, wide), BF16),
            vmem((2, TOKENS, narrow), BF16),
            vmem((2, shard, narrow), F32),
            sem((4,)),
            sem((kvh, 2)),
            sem((5,)),
            sem((kvh, nz - 1)),
            sem((kvh, nz - 1)),
            sem((kvh, nx - 1)),
            sem((kvh, nx - 1)),
            sem((kvh,)),
            sem((kvh,)),
            sem((kvh,)),
            sem((kvh,)),
            sem((kvh, nx - 1)),
            sem((kvh, nx - 1)),
            sem((kvh, nz - 1)),
            sem((kvh, nz - 1)),
            sem((max(ny - 1, 1),)),
            sem((max(ny - 1, 1),)),
            sem((max(nl - 1, 1),)),
            sem((max(nl - 1, 1),)),
            sem((nz - 1,)),
            sem((nz - 1,)),
            sem((nx - 1,)),
            sem((nx - 1,)),
            sem((1,)),
            sem((1,)),
        ],
        compiler_params=pltpu.CompilerParams(
            collective_id=0,
            has_side_effects=True,
            vmem_limit_bytes=56 * 1024 * 1024,
        ),
        cost_estimate=pl.CostEstimate(
            flops=1_400_000_000, bytes_accessed=3_000_000, transcendentals=1_400_000
        ),
    )(
        queries[0, 0],
        response_keys[0, 0],
        response_values[0, 0],
        prompt_key_rows[0],
        prompt_value_rows[0],
        upstream[0, 0],
        rewards,
        lengths,
    )
    gq, gok, gov, gpk, gpv = results
    return gq[None, None], gok[None, None], gov[None, None], gpk[None], gpv[None]


def solution(mesh, dims=(4, 4, 4, 4)):
    four = P("group", "resp", None, None)
    three = P("group", "resp", None)
    two = P("group", "resp")
    return jax.shard_map(
        functools.partial(on_device, dims),
        mesh=mesh,
        in_specs=(four, four, four, three, three, four, two, two),
        out_specs=(four, four, four, three, three),
        check_vma=False,
    )
```

time: 555 us -> 73.3 us (0.13)
  blocking collectives: 298 us -> 0 us
  waiting for transfers between devices: 199 us -> 0 us
  Pallas kernels: 0 us -> 65 us
  local copies, waits for them, and re-layouts: 26.2 us -> 5.01 us
  between operations: 16.7 us -> 1.95 us
  matrix products: 10.1 us -> 0 us
    unnamed x4 -> x0, waiting for transfers between devices: 199 us -> none
    psum x2 -> x0, blocking collectives: 196 us -> none  [the longest x1 111 us: on_device(): total = lax.psum(live_count, ('group', 'resp'))]
    all_gather x2 -> x0, blocking collectives: 101 us -> none  [the longest x1 52.6 us: on_device(): lax.all_gather(prompt_key_rows[0], 'resp', axis=0, tiled=True)]
    pallas_call x0 -> x1, Pallas kernels: none -> 65 us  [on_device(): pl.pallas_call(functools.partial(kernel, dims), out_shape=(jax.ShapeDtype...]
    unnamed x94 -> x13, local copies, waits for them, and re-layouts: 18.1 us -> 5.01 us
    dot_general x24 -> x0, matrix products: 10.1 us -> none  [the longest x4 2.38 us: on_device(): jnp.einsum('qtk,tqd->kd', probability_narrow, grad_head, preferred_elemen...]
    slice x7 -> x0, local copies, waits for them, and re-layouts: 5.75 us -> none  [the longest x1 1.45 us: on_device(): value_rows[:, lower:lower + HEAD_SIZE]]
  transfers between devices with their start and end apart: 2 -> 0, of which waited for: 2 -> 0; matrix products, arithmetic and copies ran while one was open for 2% -> 0% of each run, Pallas kernels for 0% -> 0%
where the time goes in v1:
time: 73.3 us; the launch traced here: 72 us
  Pallas kernels  65 us (89%)
  local copies, waits for them, and re-layouts  5.01 us (7%)
  between operations  1.95 us (3%)
    pallas_call x1, Pallas kernels, on_device(): pl.pallas_call(functools.partial(kernel, dims), out_shape=(jax.ShapeDtype...  65 us
    unnamed x13, local copies, waits for them, and re-layouts  5.01 us

profile of v1, /device:TPU:1, one launch (start us, length us, event | category | flops | bytes accessed | tf_op | source)
XLA Modules:
  0.0 72.0 jit_solution(16719687844164014004)
XLA Ops:
  1.9 65.0 %shard_map.119 = (bf16[128,2048]{1,0:T(8,128)(2,1)}, bf16[128,512]{1,0:T(8,128)(2,1)}, bf16[128,512]{1,0:T(8,128)(2,1)}, f32[16,512]{1,0:T(8,128)}, f32[16,512]{1,0:T(8,128)}) custom-call(bf16[128,2048]{1,0:T(8,128)(2,1)} %bitcast.16, bf16[128,512]{1,0:T(8,128)(2,1)} %bitcast.18, bf16[128,512]{1,0:T(8,128)(2,1)} %bitcast.19, bf16[16,512]{1,0:T(8,128)(2,1)} %bitcast.20, ...), custom_call_target="tpu_custom_call" | custom-call | flops 1400000000 | bytes 3000000 | tf_op jit(solution)/shard_map/pallas_call | solution.py:473
  66.9 0.0 copy-start.1
  67.0 1.9 %copy.20 = bf16[1,1,128,2048]{3,2,1,0:T(8,128)(2,1)} copy(bf16[1,1,128,2048]{3,2,1,0:T(8,128)(2,1)} %bitcast.11) | data formatting | bytes 1048576
  68.9 0.0 copy-done.1
  68.9 0.0 copy-start
  68.9 0.7 copy.21
  69.5 0.3 copy-done
  69.8 0.0 copy-start.3
  69.8 0.7 copy.22
  70.5 0.1 copy-done.3
  70.6 0.0 copy-start.2
  70.6 0.6 copy.23
  71.2 0.2 copy-done.2
  71.4 0.6 copy.24
Async XLA Ops:
  66.9 1.9 %copy-start.1 = (bf16[128,512]{1,0:T(8,128)(2,1)S(1)}, bf16[128,512]{1,0:T(8,128)(2,1)}, u32[]{:S(2)}) copy-start(bf16[128,512]{1,0:T(8,128)(2,1)} %get-tuple-element.11) | copy-start | bytes 393220
  68.9 1.0 %copy-start = (bf16[128,512]{1,0:T(8,128)(2,1)S(1)}, bf16[128,512]{1,0:T(8,128)(2,1)}, u32[]{:S(2)}) copy-start(bf16[128,512]{1,0:T(8,128)(2,1)} %get-tuple-element.12) | copy-start | bytes 393220
  69.8 0.8 %copy-start.3 = (f32[16,512]{1,0:T(8,128)S(1)}, f32[16,512]{1,0:T(8,128)}, u32[]{:S(2)}) copy-start(f32[16,512]{1,0:T(8,128)} %get-tuple-element.13) | copy-start | bytes 98308
  70.6 0.8 %copy-start.2 = (f32[16,512]{1,0:T(8,128)S(1)}, f32[16,512]{1,0:T(8,128)}, u32[]{:S(2)}) copy-start(f32[16,512]{1,0:T(8,128)} %get-tuple-element.14) | copy-start | bytes 98308

commit v2 on v1

v2 whole, which is shorter than its diff:
```python
import functools

import jax
import jax.numpy as jnp
from jax import lax
from jax.experimental import pallas as pl
from jax.experimental.pallas import tpu as pltpu
from jax.sharding import PartitionSpec as P

MESH = pl.DeviceIdType.MESH
KEY_HEADS = 4
QUERY_PER_KV = 4
HEAD = 128
TOKENS = 128
SCALE = HEAD ** (-0.5)
LOG2E = 1.4426950408889634
F32 = jnp.float32
BF16 = jnp.bfloat16
VMEM_LIMIT = 56 * 1024 * 1024


def dot(a, b, a_dim, b_dim):
    return lax.dot_general(
        a, b, (((a_dim,), (b_dim,)), ((), ())), preferred_element_type=F32
    )


def kernel(
    dims,
    q_hbm,
    ok_hbm,
    ov_hbm,
    pk_hbm,
    pv_hbm,
    up_hbm,
    reward_ref,
    length_ref,
    gq_hbm,
    gok_hbm,
    gov_hbm,
    gpk_hbm,
    gpv_hbm,
    gq_v,
    gok_v,
    gov_v,
    gpk_v,
    gpv_v,
    q_v,
    up_v,
    own_v,
    kv,
    stat,
    stat_y,
    stat_l,
    stat_z,
    stat_x,
    stat_c,
    weight_ref,
    so_ref,
    dpo_ref,
    s_ref,
    e_ref,
    dp_ref,
    pb_ref,
    ds_ref,
    acc,
    rc,
    xs,
    rx,
    zacc,
    zs,
    rz,
    in_sem,
    pin_sem,
    out_sem,
    gz_s,
    gz_r,
    gx_s,
    gx_r,
    gc_s,
    gc_r,
    sc_s,
    sc_r,
    sx_s,
    sx_r,
    sz_s,
    sz_r,
    ty_s,
    ty_r,
    tl_s,
    tl_r,
    tz_s,
    tz_r,
    tx_s,
    tx_r,
    tc_s,
    tc_r,
):
    nl, ny, nz, nx = dims
    prompt = nz * nx * 2 * 16
    rows = QUERY_PER_KV * TOKENS
    gi, ri = lax.axis_index("group"), lax.axis_index("resp")
    mc = lax.rem(ri, 2)
    mx = lax.rem(lax.div(ri, 2), nx)
    mz = lax.div(ri, 2 * nx)
    my = lax.rem(gi, ny)
    ml = lax.div(gi, ny)

    def device(c=mc, x=mx, z=mz, y=my, l=ml):
        return (l * ny + y, (z * nx + x) * 2 + c)

    def ahead(me, d, n):
        return lax.rem(me + d, n)

    def remote(src, dst, send, recv, to):
        return pltpu.make_async_remote_copy(
            src_ref=src,
            dst_ref=dst,
            send_sem=send,
            recv_sem=recv,
            device_id=to,
            device_id_type=MESH,
        )

    shard_in = []
    for g in range(KEY_HEADS):
        for i, src in enumerate((pk_hbm, pv_hbm)):
            shard_in.append(
                pltpu.make_async_copy(
                    src.at[:, g * HEAD : (g + 1) * HEAD],
                    kv.at[g, i, mc, mx, mz],
                    pin_sem.at[g, i],
                )
            )
            shard_in[-1].start()
    loads = [
        pltpu.make_async_copy(src, dst, in_sem.at[i])
        for i, (src, dst) in enumerate(
            (
                (q_hbm, q_v),
                (ok_hbm, own_v.at[0]),
                (ov_hbm, own_v.at[1]),
                (up_hbm, up_v),
            )
        )
    ]
    for load in loads:
        load.start()

    reward = reward_ref[0, 0]
    length = length_ref[0, 0]
    stat[0, 0:8] = jnp.full((8, 128), reward, F32)
    stat[0, 8:16] = jnp.full((8, 128), length.astype(F32), F32)

    partners = [device(c=1 - mc)]
    partners += [device(x=ahead(mx, d, nx)) for d in range(1, nx)]
    partners += [device(z=ahead(mz, d, nz)) for d in range(1, nz)]
    partners += [device(y=ahead(my, d, ny)) for d in range(1, ny)]
    partners += [device(l=ahead(ml, d, nl)) for d in range(1, nl)]
    barrier = pltpu.get_barrier_semaphore()
    for partner in partners:
        pl.semaphore_signal(barrier, inc=1, device_id=partner, device_id_type=MESH)
    pl.semaphore_wait(barrier, len(partners))

    def start(copies):
        for copy in copies:
            copy.start()

    def arrive(copies):
        for copy in copies:
            copy.wait_recv()

    def drain(copies):
        for copy in copies:
            copy.wait_send()

    stages = (
        ("y", my, ny, stat_y, ty_s, ty_r, False),
        ("l", ml, nl, stat_l, tl_s, tl_r, False),
        ("z", mz, nz, stat_z, tz_s, tz_r, True),
        ("x", mx, nx, stat_x, tx_s, tx_r, True),
        ("c", mc, 2, stat_c, tc_s, tc_r, True),
    )

    def stat_copies(step):
        name, me, n, into, s_sem, r_sem, _ = stages[step]
        return [
            remote(
                stat.at[step],
                into.at[d - 1],
                s_sem.at[d - 1],
                r_sem.at[d - 1],
                device(**{name: ahead(me, d, n)}),
            )
            for d in range(1, n)
        ]

    def stat_sum(step):
        arrive(stat_copies(step))
        _, _, n, into, _, _, both = stages[step]
        wins = stat[step, 0:8]
        total = stat[step, 8:16]
        for d in range(n - 1):
            total = total + into[d, 8:16]
            if both:
                wins = wins + into[d, 0:8]
        stat[step + 1, 0:8] = wins
        stat[step + 1, 8:16] = total

    def gather_z(g):
        mine = kv.at[g, :, mc, mx, mz]
        return [
            remote(
                mine,
                mine,
                gz_s.at[g, d - 1],
                gz_r.at[g, d - 1],
                device(z=ahead(mz, d, nz)),
            )
            for d in range(1, nz)
        ]

    def gather_x(g):
        mine = kv.at[g, :, mc, mx]
        return [
            remote(
                mine,
                mine,
                gx_s.at[g, d - 1],
                gx_r.at[g, d - 1],
                device(x=ahead(mx, d, nx)),
            )
            for d in range(1, nx)
        ]

    def gather_c(g):
        mine = kv.at[g, :, mc]
        return [remote(mine, mine, gc_s.at[g], gc_r.at[g], device(c=1 - mc))]

    def reduce_c(g):
        return [
            remote(
                acc.at[g, :, 1 - mc],
                rc.at[g],
                sc_s.at[g],
                sc_r.at[g],
                device(c=1 - mc),
            )
        ]

    def reduce_x(g):
        return [
            remote(
                xs.at[g, :, ahead(mx, d, nx)],
                rx.at[g, d - 1],
                sx_s.at[g, d - 1],
                sx_r.at[g, d - 1],
                device(x=ahead(mx, d, nx)),
            )
            for d in range(1, nx)
        ]

    def reduce_z(g):
        return [
            remote(
                zs.at[g, :, ahead(mz, d, nz)],
                rz.at[g, d - 1],
                sz_s.at[g, d - 1],
                sz_r.at[g, d - 1],
                device(z=ahead(mz, d, nz)),
            )
            for d in range(1, nz)
        ]

    def after_c(g):
        arrive(reduce_c(g))
        xs[g] = (acc[g, :, mc] + rc[g]).astype(BF16)
        start(reduce_x(g))

    def after_x(g):
        arrive(reduce_x(g))
        part = acc[g, :, mc, mx] + rc[g, :, mx]
        for d in range(nx - 1):
            part = part + rx[g, d].astype(F32)
        zacc[g] = part
        zs[g] = part.astype(BF16)
        start(reduce_z(g))

    def after_z(g):
        arrive(reduce_z(g))
        part = zacc[g, :, mz]
        for d in range(nz - 1):
            part = part + rz[g, d].astype(F32)
        gpk_v[:, g * HEAD : (g + 1) * HEAD] = part[0]
        gpv_v[:, g * HEAD : (g + 1) * HEAD] = part[1]

    def head_cols(g):
        return pl.ds(pl.multiple_of(g * HEAD, HEAD), HEAD)

    def query_cols(g, j):
        return pl.ds(pl.multiple_of((g * QUERY_PER_KV + j) * HEAD, HEAD), HEAD)

    def stacked(ref, g):
        return jnp.concatenate(
            [ref[:, query_cols(g, j)] for j in range(QUERY_PER_KV)], axis=0
        )

    def own_part(g, carry):
        key = lax.broadcasted_iota(jnp.int32, (TOKENS, rows), 0)
        step = lax.broadcasted_iota(jnp.int32, (TOKENS, rows), 1) & (TOKENS - 1)
        scores = dot(own_v[0, :, head_cols(g)], stacked(q_v, g), 1, 1)
        so_ref[g] = jnp.where(key <= step, scores, -1e30)
        step = lax.broadcasted_iota(jnp.int32, (TOKENS, HEAD), 0)
        live = jnp.where(step < length, 1.0, 0.0)
        for j in range(QUERY_PER_KV):
            cols = query_cols(g, j)
            up_v[:, cols] = (up_v[:, cols].astype(F32) * live).astype(BF16)
        dpo_ref[g] = dot(own_v[1, :, head_cols(g)], stacked(up_v, g), 1, 1)
        return carry

    def forward(g):
        s_ref[...] = dot(kv[g, 0].reshape(prompt, HEAD), stacked(q_v, g), 1, 1)
        top = jnp.maximum(
            jnp.max(s_ref[...], axis=0, keepdims=True),
            jnp.max(so_ref[g], axis=0, keepdims=True),
        )
        e_ref[0:prompt] = jnp.exp2((s_ref[...] - top) * (SCALE * LOG2E))
        e_ref[prompt:] = jnp.exp2((so_ref[g] - top) * (SCALE * LOG2E))
        inverse = 1.0 / jnp.sum(e_ref[...], axis=0, keepdims=True)
        pb_ref[...] = (e_ref[...] * inverse).astype(BF16)
        return inverse

    def backward(g, inverse):
        grad_out = stacked(up_v, g)
        dp_ref[0:prompt] = dot(kv[g, 1].reshape(prompt, HEAD), grad_out, 1, 1)
        dp_ref[prompt:] = dpo_ref[g]
        weight = weight_ref[0:1]
        grad_values = weight * dot(pb_ref[...], grad_out, 1, 0)
        acc[g, 1] = grad_values[0:prompt].reshape(2, nx, nz, 16, HEAD)
        gov_v[:, head_cols(g)] = grad_values[prompt:].astype(BF16)
        delta = jnp.sum(pb_ref[...].astype(F32) * dp_ref[...], axis=0, keepdims=True)
        ds_ref[...] = ((e_ref[...] * inverse) * (dp_ref[...] - delta)).astype(BF16)
        grad_keys = (weight * SCALE) * dot(ds_ref[...], stacked(q_v, g), 1, 0)
        acc[g, 0] = grad_keys[0:prompt].reshape(2, nx, nz, 16, HEAD)
        gok_v[:, head_cols(g)] = grad_keys[prompt:].astype(BF16)

    def query_gradient(g):
        keys = kv[g, 0].reshape(prompt, HEAD)
        turned = dot(keys, ds_ref[0:prompt], 0, 0) + dot(
            own_v[0, :, head_cols(g)], ds_ref[prompt:], 0, 0
        )
        weight = weight_ref[0:1] * SCALE
        for j in range(QUERY_PER_KV):
            block = turned[:, j * TOKENS : (j + 1) * TOKENS]
            gq_v[:, query_cols(g, j)] = (block.T * weight).astype(BF16)

    start(stat_copies(0))
    for copy in shard_in[0:2]:
        copy.wait()
    start(gather_z(0))
    for g in range(1, KEY_HEADS):
        for copy in shard_in[2 * g : 2 * g + 2]:
            copy.wait()
        start(gather_z(g))
    for load in loads:
        load.wait()
    lax.fori_loop(0, KEY_HEADS, own_part, 0)
    stat_sum(0)
    start(stat_copies(1))
    arrive(gather_z(0))
    start(gather_x(0))
    arrive(gather_z(1))
    start(gather_x(1))
    stat_sum(1)
    start(stat_copies(2))
    arrive(gather_x(0))
    start(gather_c(0))
    stat_sum(2)
    start(stat_copies(3))

    def head(g, carry):
        arrive(gather_c(g))
        inverse = forward(g)

        @pl.when(g + 2 < KEY_HEADS)
        def _():
            arrive(gather_z(g + 2))
            start(gather_x(g + 2))

        @pl.when(g + 1 < KEY_HEADS)
        def _():
            arrive(gather_x(g + 1))
            start(gather_c(g + 1))

        @pl.when(g == 0)
        def _():
            stat_sum(3)
            start(stat_copies(4))
            stat_sum(4)
            advantage = reward - stat[5, 0:8] / (nz * nx * 2)
            weight_ref[...] = advantage / stat[5, 8:16]

        @pl.when(g > 0)
        def _():
            after_c(g - 1)

        backward(g, inverse)
        start(reduce_c(g))

        @pl.when(g > 0)
        def _():
            after_x(g - 1)

        query_gradient(g)
        return carry

    lax.fori_loop(0, KEY_HEADS, head, 0)
    stores = [
        pltpu.make_async_copy(src, dst, out_sem.at[i])
        for i, (src, dst) in enumerate(
            (
                (gq_v, gq_hbm),
                (gok_v, gok_hbm),
                (gov_v, gov_hbm),
                (gpk_v, gpk_hbm),
                (gpv_v, gpv_hbm),
            )
        )
    ]
    last = KEY_HEADS - 1
    after_c(last)
    start(stores[0:3])
    for g in range(last):
        after_z(g)
    after_x(last)
    after_z(last)
    start(stores[3:5])
    for step in range(len(stages)):
        drain(stat_copies(step))
    for g in range(KEY_HEADS):
        for copies in (gather_z, gather_x, gather_c, reduce_c, reduce_x, reduce_z):
            drain(copies(g))
    for store in stores:
        store.wait()


def store_kernel(*refs):
    count = len(refs) // 2
    sem = refs[-1]
    copies = [
        pltpu.make_async_copy(refs[i], refs[count + i], sem.at[i])
        for i in range(count)
    ]
    for copy in copies:
        copy.start()
    for copy in copies:
        copy.wait()


def on_device(
    dims,
    queries,
    response_keys,
    response_values,
    prompt_key_rows,
    prompt_value_rows,
    upstream,
    rewards,
    lengths,
):
    nl, ny, nz, nx = dims
    kvh, rows = KEY_HEADS, QUERY_PER_KV * TOKENS
    prompt = nz * nx * 2 * 16
    joined = prompt + TOKENS
    wide, narrow = queries.shape[3], response_keys.shape[3]
    shard = prompt_key_rows.shape[1]
    vmem, sem = pltpu.VMEM, pltpu.SemaphoreType.DMA
    anywhere = pl.BlockSpec(memory_space=pl.ANY)
    scalar = pl.BlockSpec(memory_space=pltpu.SMEM)
    shapes = (
        jax.ShapeDtypeStruct((TOKENS, wide), BF16),
        jax.ShapeDtypeStruct((TOKENS, narrow), BF16),
        jax.ShapeDtypeStruct((TOKENS, narrow), BF16),
        jax.ShapeDtypeStruct((shard, narrow), F32),
        jax.ShapeDtypeStruct((shard, narrow), F32),
    )
    results = pl.pallas_call(
        functools.partial(kernel, dims),
        out_shape=shapes,
        in_specs=[anywhere] * 6 + [scalar] * 2,
        out_specs=[anywhere] * 5,
        scratch_shapes=[
            vmem((TOKENS, wide), BF16),
            vmem((TOKENS, narrow), BF16),
            vmem((TOKENS, narrow), BF16),
            vmem((shard, narrow), F32),
            vmem((shard, narrow), F32),
            vmem((TOKENS, wide), BF16),
            vmem((TOKENS, wide), BF16),
            vmem((2, TOKENS, narrow), BF16),
            vmem((kvh, 2, 2, nx, nz, 16, HEAD), BF16),
            vmem((6, 16, 128), F32),
            vmem((max(ny - 1, 1), 16, 128), F32),
            vmem((max(nl - 1, 1), 16, 128), F32),
            vmem((max(nz - 1, 1), 16, 128), F32),
            vmem((max(nx - 1, 1), 16, 128), F32),
            vmem((1, 16, 128), F32),
            vmem((8, 128), F32),
            vmem((kvh, TOKENS, rows), F32),
            vmem((kvh, TOKENS, rows), F32),
            vmem((prompt, rows), F32),
            vmem((joined, rows), F32),
            vmem((joined, rows), F32),
            vmem((joined, rows), BF16),
            vmem((joined, rows), BF16),
            vmem((kvh, 2, 2, nx, nz, 16, HEAD), F32),
            vmem((kvh, 2, nx, nz, 16, HEAD), F32),
            vmem((kvh, 2, nx, nz, 16, HEAD), BF16),
            vmem((kvh, nx - 1, 2, nz, 16, HEAD), BF16),
            vmem((kvh, 2, nz, 16, HEAD), F32),
            vmem((kvh, 2, nz, 16, HEAD), BF16),
            vmem((kvh, nz - 1, 2, 16, HEAD), BF16),
            sem((4,)),
            sem((kvh, 2)),
            sem((5,)),
            sem((kvh, nz - 1)),
            sem((kvh, nz - 1)),
            sem((kvh, nx - 1)),
            sem((kvh, nx - 1)),
            sem((kvh,)),
            sem((kvh,)),
            sem((kvh,)),
            sem((kvh,)),
            sem((kvh, nx - 1)),
            sem((kvh, nx - 1)),
            sem((kvh, nz - 1)),
            sem((kvh, nz - 1)),
            sem((max(ny - 1, 1),)),
            sem((max(ny - 1, 1),)),
            sem((max(nl - 1, 1),)),
            sem((max(nl - 1, 1),)),
            sem((nz - 1,)),
            sem((nz - 1,)),
            sem((nx - 1,)),
            sem((nx - 1,)),
            sem((1,)),
            sem((1,)),
        ],
        compiler_params=pltpu.CompilerParams(
            collective_id=0,
            has_side_effects=True,
            vmem_limit_bytes=VMEM_LIMIT,
        ),
        cost_estimate=pl.CostEstimate(
            flops=1_400_000_000, bytes_accessed=3_000_000, transcendentals=1_400_000
        ),
    )(
        queries[0, 0],
        response_keys[0, 0],
        response_values[0, 0],
        prompt_key_rows[0],
        prompt_value_rows[0],
        upstream[0, 0],
        rewards,
        lengths,
    )
    gq, gok, gov, gpk, gpv = pl.pallas_call(
        store_kernel,
        out_shape=shapes,
        in_specs=[anywhere] * 5,
        out_specs=[anywhere] * 5,
        scratch_shapes=[sem((5,))],
        compiler_params=pltpu.CompilerParams(vmem_limit_bytes=VMEM_LIMIT),
    )(*results)
    return gq[None, None], gok[None, None], gov[None, None], gpk[None], gpv[None]


def solution(mesh, dims=(4, 4, 4, 4)):
    four = P("group", "resp", None, None)
    three = P("group", "resp", None)
    two = P("group", "resp")
    return jax.shard_map(
        functools.partial(on_device, dims),
        mesh=mesh,
        in_specs=(four, four, four, three, three, four, two, two),
        out_specs=(four, four, four, three, three),
        check_vma=False,
    )
```

time: 73.3 us -> 99.5 us (1.36)
  the two profiles are of different devices: /device:TPU:1 before, /device:TPU:24 now
where the time goes in v2:
time: 99.5 us; the launch traced here: 99.3 us
  Pallas kernels  97.4 us (98%)
  between operations  1.93 us (2%)
    pallas_call x1, Pallas kernels, on_device(): pl.pallas_call(functools.partial(kernel, dims), out_shape=shapes, in_spec...  70.4 us
    pallas_call x1, Pallas kernels, on_device(): pl.pallas_call(store_kernel, out_shape=shapes, in_specs=[anywhere] * 5, o...  27 us

profile of v2, /device:TPU:24, one launch (start us, length us, event | category | flops | bytes accessed | tf_op | source)
XLA Modules:
  0.0 99.3 jit_solution(7796202716981458101)
XLA Ops:
  1.9 70.4 %shard_map.119 = (bf16[128,2048]{1,0:T(8,128)(2,1)}, bf16[128,512]{1,0:T(8,128)(2,1)}, bf16[128,512]{1,0:T(8,128)(2,1)}, f32[16,512]{1,0:T(8,128)}, f32[16,512]{1,0:T(8,128)}) custom-call(bf16[128,2048]{1,0:T(8,128)(2,1)} %bitcast.11, bf16[128,512]{1,0:T(8,128)(2,1)} %bitcast.14, bf16[128,512]{1,0:T(8,128)(2,1)} %bitcast.15, bf16[16,512]{1,0:T(8,128)(2,1)} %bitcast.20, ...), custom_call_target="tpu_custom_call" | custom-call | flops 1400000000 | bytes 3000000 | tf_op jit(solution)/shard_map/pallas_call | solution.py:487
  72.4 27.0 %shard_map.120 = (bf16[128,2048]{1,0:T(8,128)(2,1)}, bf16[128,512]{1,0:T(8,128)(2,1)}, bf16[128,512]{1,0:T(8,128)(2,1)}, f32[16,512]{1,0:T(8,128)}, f32[16,512]{1,0:T(8,128)}) custom-call(bf16[128,2048]{1,0:T(8,128)(2,1)} %get-tuple-element.15.refs_0_, bf16[128,512]{1,0:T(8,128)(2,1)} %get-tuple-element.16.refs_1_, ...), custom_call_target="tpu_custom_call" | custom-call | tf_op jit(solution)/shard_map/pallas_call | solution.py:567

commit v3 on v2

v3 whole, which is shorter than its diff:
```python
import functools

import jax
import jax.numpy as jnp
from jax import lax
from jax.experimental import pallas as pl
from jax.experimental.pallas import tpu as pltpu
from jax.sharding import PartitionSpec as P

MESH = pl.DeviceIdType.MESH
KEY_HEADS = 4
QUERY_PER_KV = 4
HEAD = 128
TOKENS = 128
SCALE = HEAD ** (-0.5)
LOG2E = 1.4426950408889634
F32 = jnp.float32
BF16 = jnp.bfloat16
VMEM_LIMIT = 56 * 1024 * 1024


def dot(a, b, a_dim, b_dim):
    return lax.dot_general(
        a, b, (((a_dim,), (b_dim,)), ((), ())), preferred_element_type=F32
    )


def kernel(
    dims,
    q_hbm,
    ok_hbm,
    ov_hbm,
    pk_hbm,
    pv_hbm,
    up_hbm,
    reward_ref,
    length_ref,
    gq_hbm,
    gok_hbm,
    gov_hbm,
    gpk_hbm,
    gpv_hbm,
    gq_v,
    go_v,
    gp_v,
    q_v,
    up_v,
    own_v,
    shard_v,
    kv,
    stat,
    stat_in,
    own_grad,
    so_ref,
    dpo_ref,
    s_ref,
    e_ref,
    dp_ref,
    pb_ref,
    ds_ref,
    acc,
    cs,
    rc,
    part,
    xs,
    rx,
    zs,
    rz,
    in_sem,
    out_sem,
    gz_s,
    gz_r,
    gx_s,
    gx_r,
    gc_s,
    gc_r,
    sc_s,
    sc_r,
    sx_s,
    sx_r,
    sz_s,
    sz_r,
    t_s,
    t_r,
):
    nl, ny, nz, nx = dims
    prompt = nz * nx * 2 * 16
    rows = QUERY_PER_KV * TOKENS
    gi, ri = lax.axis_index("group"), lax.axis_index("resp")
    mc = lax.rem(ri, 2)
    mx = lax.rem(lax.div(ri, 2), nx)
    mz = lax.div(ri, 2 * nx)
    my = lax.rem(gi, ny)
    ml = lax.div(gi, ny)

    def device(c=mc, x=mx, z=mz, y=my, l=ml):
        return (l * ny + y, (z * nx + x) * 2 + c)

    def ahead(me, d, n):
        return lax.rem(me + d, n)

    def remote(src, dst, send, recv, to):
        return pltpu.make_async_remote_copy(
            src_ref=src,
            dst_ref=dst,
            send_sem=send,
            recv_sem=recv,
            device_id=to,
            device_id_type=MESH,
        )

    on_core = device(c=1 - mc)
    on_x = [device(x=ahead(mx, d, nx)) for d in range(1, nx)]
    on_z = [device(z=ahead(mz, d, nz)) for d in range(1, nz)]
    on_y = [device(y=ahead(my, d, ny)) for d in range(1, ny)]
    on_l = [device(l=ahead(ml, d, nl)) for d in range(1, nl)]
    partners = [on_core] + on_x + on_z + on_y + on_l
    barrier = pltpu.get_barrier_semaphore()
    for partner in partners:
        pl.semaphore_signal(barrier, inc=1, device_id=partner, device_id_type=MESH)

    loads = [
        pltpu.make_async_copy(src, dst, in_sem.at[i])
        for i, (src, dst) in enumerate(
            (
                (pk_hbm, shard_v.at[0]),
                (pv_hbm, shard_v.at[1]),
                (q_hbm, q_v),
                (ok_hbm, own_v.at[0]),
                (ov_hbm, own_v.at[1]),
                (up_hbm, up_v),
            )
        )
    ]
    for load in loads:
        load.start()

    reward = reward_ref[0, 0]
    length = length_ref[0, 0]
    stat[0, 0:8] = jnp.full((8, 128), reward, F32)
    stat[0, 8:16] = jnp.full((8, 128), length.astype(F32), F32)

    def start(copies):
        for copy in copies:
            copy.start()

    def arrive(copies):
        for copy in copies:
            copy.wait_recv()

    def drain(copies):
        for copy in copies:
            copy.wait_send()

    stages = (on_z, on_x, [on_core], on_y, on_l)

    def stat_copies(step):
        return [
            remote(
                stat.at[step],
                stat_in.at[step, d],
                t_s.at[step, d],
                t_r.at[step, d],
                to,
            )
            for d, to in enumerate(stages[step])
        ]

    def stat_sum(step):
        arrive(stat_copies(step))
        total = stat[step]
        for d in range(len(stages[step])):
            total = total + stat_in[step, d]
        stat[step + 1] = total

    def gather_z():
        mine = kv.at[:, mc, mx, mz]
        return [
            remote(mine, mine, gz_s.at[d], gz_r.at[d], to) for d, to in enumerate(on_z)
        ]

    def gather_x(half):
        mine = kv.at[2 * half : 2 * half + 2, mc, mx]
        return [
            remote(mine, mine, gx_s.at[half, d], gx_r.at[half, d], to)
            for d, to in enumerate(on_x)
        ]

    def gather_c(half):
        mine = kv.at[2 * half : 2 * half + 2, mc]
        return [remote(mine, mine, gc_s.at[half], gc_r.at[half], on_core)]

    chunks = (slice(0, 2), slice(2, 3), slice(3, 4))

    def reduce_c(n):
        return [
            remote(cs.at[chunks[n]], rc.at[chunks[n]], sc_s.at[n], sc_r.at[n], on_core)
        ]

    def reduce_x(n):
        return [
            remote(
                xs.at[chunks[n], ahead(mx, d + 1, nx)],
                rx.at[d, chunks[n]],
                sx_s.at[n, d],
                sx_r.at[n, d],
                to,
            )
            for d, to in enumerate(on_x)
        ]

    def reduce_z(n):
        return [
            remote(
                zs.at[chunks[n], ahead(mz, d + 1, nz)],
                rz.at[d, chunks[n]],
                sz_s.at[n, d],
                sz_r.at[n, d],
                to,
            )
            for d, to in enumerate(on_z)
        ]

    def before_c(n):
        cs[chunks[n]] = acc[chunks[n], 1 - mc].astype(BF16)
        start(reduce_c(n))

    def after_c(n):
        arrive(reduce_c(n))
        both = acc[chunks[n], mc] + rc[chunks[n]].astype(F32)
        part[chunks[n]] = both
        xs[chunks[n]] = both.astype(BF16)
        start(reduce_x(n))

    def after_x(n):
        arrive(reduce_x(n))
        both = part[chunks[n], mx]
        for d in range(nx - 1):
            both = both + rx[d, chunks[n]].astype(F32)
        part[chunks[n], 0] = both
        zs[chunks[n]] = both.astype(BF16)
        start(reduce_z(n))

    def after_z(n, scale):
        arrive(reduce_z(n))
        both = part[chunks[n], 0, mz]
        for d in range(nz - 1):
            both = both + rz[d, chunks[n]].astype(F32)
        for i, g in enumerate(range(chunks[n].start, chunks[n].stop)):
            gp_v[0, :, head_cols(g)] = both[i, 0] * scale
            gp_v[1, :, head_cols(g)] = both[i, 1] * scale

    def head_cols(g):
        return slice(g * HEAD, (g + 1) * HEAD)

    def query_cols(g, j):
        lower = (g * QUERY_PER_KV + j) * HEAD
        return slice(lower, lower + HEAD)

    def stacked(ref, g):
        return jnp.concatenate(
            [ref[:, query_cols(g, j)] for j in range(QUERY_PER_KV)], axis=0
        )

    def prompt_rows(g, i):
        return kv[g, :, :, :, i].reshape(prompt, HEAD)

    def own_part(g):
        key = lax.broadcasted_iota(jnp.int32, (TOKENS, rows), 0)
        step = lax.broadcasted_iota(jnp.int32, (TOKENS, rows), 1) & (TOKENS - 1)
        scores = dot(own_v[0, :, head_cols(g)], stacked(q_v, g), 1, 1)
        so_ref[g] = jnp.where(key <= step, scores, -1e30)
        step = lax.broadcasted_iota(jnp.int32, (TOKENS, HEAD), 0)
        live = jnp.where(step < length, 1.0, 0.0)
        for j in range(QUERY_PER_KV):
            cols = query_cols(g, j)
            up_v[:, cols] = (up_v[:, cols].astype(F32) * live).astype(BF16)
        dpo_ref[g] = dot(own_v[1, :, head_cols(g)], stacked(up_v, g), 1, 1)

    def attend(g, advantage):
        q_g, grad_out = stacked(q_v, g), stacked(up_v, g)
        s_ref[...] = dot(prompt_rows(g, 0), q_g, 1, 1)
        dp_ref[0:prompt] = dot(prompt_rows(g, 1), grad_out, 1, 1)
        dp_ref[prompt:] = dpo_ref[g]
        top = jnp.maximum(
            jnp.max(s_ref[...], axis=0, keepdims=True),
            jnp.max(so_ref[g], axis=0, keepdims=True),
        )
        e_ref[0:prompt] = jnp.exp2((s_ref[...] - top) * (SCALE * LOG2E))
        e_ref[prompt:] = jnp.exp2((so_ref[g] - top) * (SCALE * LOG2E))
        inverse = 1.0 / jnp.sum(e_ref[...], axis=0, keepdims=True)
        pb_ref[...] = (e_ref[...] * inverse).astype(BF16)
        grad_values = advantage * dot(pb_ref[...], grad_out, 1, 0)
        acc[g, :, :, :, 1] = grad_values[0:prompt].reshape(2, nx, nz, 16, HEAD)
        own_grad[1, :, head_cols(g)] = grad_values[prompt:]
        delta = jnp.sum(pb_ref[...].astype(F32) * dp_ref[...], axis=0, keepdims=True)
        ds_ref[g] = ((e_ref[...] * inverse) * (dp_ref[...] - delta)).astype(BF16)
        grad_keys = (advantage * SCALE) * dot(ds_ref[g], q_g, 1, 0)
        acc[g, :, :, :, 0] = grad_keys[0:prompt].reshape(2, nx, nz, 16, HEAD)
        own_grad[0, :, head_cols(g)] = grad_keys[prompt:]

    def query_gradient(g, weight):
        turned = dot(prompt_rows(g, 0), ds_ref[g, 0:prompt], 0, 0) + dot(
            own_v[0, :, head_cols(g)], ds_ref[g, prompt:], 0, 0
        )
        for j in range(QUERY_PER_KV):
            block = turned[:, j * TOKENS : (j + 1) * TOKENS]
            gq_v[:, query_cols(g, j)] = (block.T * weight).astype(BF16)

    loads[0].wait()
    loads[1].wait()
    for g in range(KEY_HEADS):
        kv[g, mc, mx, mz, 0] = shard_v[0, :, head_cols(g)]
        kv[g, mc, mx, mz, 1] = shard_v[1, :, head_cols(g)]
    pl.semaphore_wait(barrier, len(partners))
    start(gather_z())
    start(stat_copies(0))
    for load in loads[2:]:
        load.wait()
    own_part(0)
    own_part(1)
    arrive(gather_z())
    start(gather_x(0))
    start(gather_x(1))
    stat_sum(0)
    start(stat_copies(1))
    own_part(2)
    own_part(3)
    arrive(gather_x(0))
    start(gather_c(0))
    stat_sum(1)
    start(stat_copies(2))
    arrive(gather_x(1))
    start(gather_c(1))
    stat_sum(2)
    start(stat_copies(3))
    advantage = reward - stat[3, 0:1] / (nz * nx * 2)
    arrive(gather_c(0))
    attend(0, advantage)
    attend(1, advantage)
    before_c(0)
    arrive(gather_c(1))
    attend(2, advantage)
    before_c(1)
    after_c(0)
    stat_sum(3)
    start(stat_copies(4))
    attend(3, advantage)
    before_c(2)
    after_c(1)
    after_x(0)
    after_c(2)
    stat_sum(4)
    unit = 1.0 / stat[5, 8:9]
    weight = advantage * SCALE * unit
    query_gradient(0, weight)
    after_x(1)
    query_gradient(1, weight)
    after_x(2)
    query_gradient(2, weight)
    query_gradient(3, weight)
    for g in range(KEY_HEADS):
        for i in range(2):
            go_v[i, :, head_cols(g)] = (own_grad[i, :, head_cols(g)] * unit).astype(BF16)
    stores = [
        pltpu.make_async_copy(src, dst, out_sem.at[i])
        for i, (src, dst) in enumerate(
            (
                (gq_v, gq_hbm),
                (go_v.at[0], gok_hbm),
                (go_v.at[1], gov_hbm),
                (gp_v.at[0], gpk_hbm),
                (gp_v.at[1], gpv_hbm),
            )
        )
    ]
    start(stores[0:3])
    after_z(0, unit)
    after_z(1, unit)
    after_z(2, unit)
    start(stores[3:5])
    for step in range(len(stages)):
        drain(stat_copies(step))
    drain(gather_z())
    for half in range(2):
        drain(gather_x(half))
        drain(gather_c(half))
    for n in range(len(chunks)):
        drain(reduce_c(n))
        drain(reduce_x(n))
        drain(reduce_z(n))
    for store in stores:
        store.wait()


def store_kernel(*refs):
    sources, targets, holds = refs[0:5], refs[5:10], refs[10:15]
    in_sem, out_sem = refs[15:17]
    ins = [
        pltpu.make_async_copy(sources[i], holds[i], in_sem.at[i]) for i in range(5)
    ]
    outs = [
        pltpu.make_async_copy(holds[i], targets[i], out_sem.at[i]) for i in range(5)
    ]
    for copy in ins:
        copy.start()
    for i in (1, 2, 3, 4, 0):
        ins[i].wait()
        outs[i].start()
    for copy in outs:
        copy.wait()


def on_device(
    dims,
    queries,
    response_keys,
    response_values,
    prompt_key_rows,
    prompt_value_rows,
    upstream,
    rewards,
    lengths,
):
    nl, ny, nz, nx = dims
    kvh, rows = KEY_HEADS, QUERY_PER_KV * TOKENS
    prompt = nz * nx * 2 * 16
    joined = prompt + TOKENS
    wide, narrow = queries.shape[3], response_keys.shape[3]
    shard = prompt_key_rows.shape[1]
    most = max(dims) - 1
    vmem, sem = pltpu.VMEM, pltpu.SemaphoreType.DMA
    anywhere = pl.BlockSpec(memory_space=pl.ANY)
    scalar = pl.BlockSpec(memory_space=pltpu.SMEM)
    shapes = (
        jax.ShapeDtypeStruct((TOKENS, wide), BF16),
        jax.ShapeDtypeStruct((TOKENS, narrow), BF16),
        jax.ShapeDtypeStruct((TOKENS, narrow), BF16),
        jax.ShapeDtypeStruct((shard, narrow), F32),
        jax.ShapeDtypeStruct((shard, narrow), F32),
    )
    results = pl.pallas_call(
        functools.partial(kernel, dims),
        out_shape=shapes,
        in_specs=[anywhere] * 6 + [scalar] * 2,
        out_specs=[anywhere] * 5,
        scratch_shapes=[
            vmem((TOKENS, wide), BF16),
            vmem((2, TOKENS, narrow), BF16),
            vmem((2, shard, narrow), F32),
            vmem((TOKENS, wide), BF16),
            vmem((TOKENS, wide), BF16),
            vmem((2, TOKENS, narrow), BF16),
            vmem((2, shard, narrow), BF16),
            vmem((kvh, 2, nx, nz, 2, 16, HEAD), BF16),
            vmem((6, 16, 128), F32),
            vmem((5, most, 16, 128), F32),
            vmem((2, TOKENS, narrow), F32),
            vmem((kvh, TOKENS, rows), F32),
            vmem((kvh, TOKENS, rows), F32),
            vmem((prompt, rows), F32),
            vmem((joined, rows), F32),
            vmem((joined, rows), F32),
            vmem((joined, rows), BF16),
            vmem((kvh, joined, rows), BF16),
            vmem((kvh, 2, nx, nz, 2, 16, HEAD), F32),
            vmem((kvh, nx, nz, 2, 16, HEAD), BF16),
            vmem((kvh, nx, nz, 2, 16, HEAD), BF16),
            vmem((kvh, nx, nz, 2, 16, HEAD), F32),
            vmem((kvh, nx, nz, 2, 16, HEAD), BF16),
            vmem((nx - 1, kvh, nz, 2, 16, HEAD), BF16),
            vmem((kvh, nz, 2, 16, HEAD), BF16),
            vmem((nz - 1, kvh, 2, 16, HEAD), BF16),
            sem((6,)),
            sem((5,)),
            sem((nz - 1,)),
            sem((nz - 1,)),
            sem((2, nx - 1)),
            sem((2, nx - 1)),
            sem((2,)),
            sem((2,)),
            sem((3,)),
            sem((3,)),
            sem((3, nx - 1)),
            sem((3, nx - 1)),
            sem((3, nz - 1)),
            sem((3, nz - 1)),
            sem((5, most)),
            sem((5, most)),
        ],
        compiler_params=pltpu.CompilerParams(
            collective_id=0,
            has_side_effects=True,
            vmem_limit_bytes=VMEM_LIMIT,
        ),
        cost_estimate=pl.CostEstimate(
            flops=1_400_000_000, bytes_accessed=3_000_000, transcendentals=1_400_000
        ),
    )(
        queries[0, 0],
        response_keys[0, 0],
        response_values[0, 0],
        prompt_key_rows[0],
        prompt_value_rows[0],
        upstream[0, 0],
        rewards,
        lengths,
    )
    gq, gok, gov, gpk, gpv = pl.pallas_call(
        store_kernel,
        out_shape=shapes,
        in_specs=[anywhere] * 5,
        out_specs=[anywhere] * 5,
        scratch_shapes=[vmem(x.shape, x.dtype) for x in shapes] + [sem((5,)), sem((5,))],
        compiler_params=pltpu.CompilerParams(vmem_limit_bytes=VMEM_LIMIT),
    )(*results)
    return gq[None, None], gok[None, None], gov[None, None], gpk[None], gpv[None]


def solution(mesh, dims=(4, 4, 4, 4)):
    four = P("group", "resp", None, None)
    three = P("group", "resp", None)
    two = P("group", "resp")
    return jax.shard_map(
        functools.partial(on_device, dims),
        mesh=mesh,
        in_specs=(four, four, four, three, three, four, two, two),
        out_specs=(four, four, four, three, three),
        check_vma=False,
    )
```

time: 99.5 us -> 61 us (0.61)
  the two profiles are of different devices: /device:TPU:24 before, /device:TPU:1 now
where the time goes in v3:
time: 61 us; the launch traced here: 60.2 us
  Pallas kernels  58.3 us (96%)
  between operations  1.93 us (3%)
    pallas_call x1, Pallas kernels, on_device(): pl.pallas_call(functools.partial(kernel, dims), out_shape=shapes, in_spec...  56.2 us
    pallas_call x1, Pallas kernels, on_device(): pl.pallas_call(store_kernel, out_shape=shapes, in_specs=[anywhere] * 5, o...  2.06 us

profile of v3, /device:TPU:1, one launch (start us, length us, event | category | flops | bytes accessed | tf_op | source)
XLA Modules:
  0.0 60.2 jit_solution(18383005100993783919)
XLA Ops:
  1.9 56.2 %shard_map.119 = (bf16[128,2048]{1,0:T(8,128)(2,1)}, bf16[128,512]{1,0:T(8,128)(2,1)}, bf16[128,512]{1,0:T(8,128)(2,1)}, f32[16,512]{1,0:T(8,128)}, f32[16,512]{1,0:T(8,128)}) custom-call(bf16[128,2048]{1,0:T(8,128)(2,1)} %bitcast.11, bf16[128,512]{1,0:T(8,128)(2,1)} %bitcast.14, bf16[128,512]{1,0:T(8,128)(2,1)} %bitcast.15, bf16[16,512]{1,0:T(8,128)(2,1)} %bitcast.20, ...), custom_call_target="tpu_custom_call" | custom-call | flops 1400000000 | bytes 3000000 | tf_op jit(solution)/shard_map/pallas_call | solution.py:442
  58.1 2.1 %shard_map.120 = (bf16[128,2048]{1,0:T(8,128)(2,1)}, bf16[128,512]{1,0:T(8,128)(2,1)}, bf16[128,512]{1,0:T(8,128)(2,1)}, f32[16,512]{1,0:T(8,128)}, f32[16,512]{1,0:T(8,128)}) custom-call(bf16[128,2048]{1,0:T(8,128)(2,1)} %get-tuple-element.15.refs_0_, bf16[128,512]{1,0:T(8,128)(2,1)} %get-tuple-element.16.refs_1_, ...), custom_call_target="tpu_custom_call" | custom-call | tf_op jit(solution)/shard_map/pallas_call | solution.py:509

commit v4 on v3

--- a/solution.py
+++ b/solution.py
@@ -70,8 +70,12 @@
     out_sem,
     gz_s,
     gz_r,
+    hz_s,
+    hz_r,
     gx_s,
     gx_r,
+    hx_s,
+    hx_r,
     gc_s,
     gc_r,
     sc_s,
@@ -109,12 +113,22 @@
             device_id_type=MESH,
         )
 
+    def ring(me, n):
+        return [lax.rem(me + 1, n)] + ([lax.rem(me + n - 1, n)] if n > 2 else [])
+
+    def pairs(me, n):
+        flip = [me + 1 - 2 * lax.rem(me, 2)] if n > 1 else []
+        return flip + ([n - 1 - me] if n > 2 else [])
+
+    near_z, near_x = ring(mz, nz), ring(mx, nx)
     on_core = device(c=1 - mc)
+    next_z = [device(z=z) for z in near_z]
+    next_x = [device(x=x) for x in near_x]
+    pair_y = [device(y=y) for y in pairs(my, ny)]
+    pair_l = [device(l=l) for l in pairs(ml, nl)]
     on_x = [device(x=ahead(mx, d, nx)) for d in range(1, nx)]
     on_z = [device(z=ahead(mz, d, nz)) for d in range(1, nz)]
-    on_y = [device(y=ahead(my, d, ny)) for d in range(1, ny)]
-    on_l = [device(l=ahead(ml, d, nl)) for d in range(1, nl)]
-    partners = [on_core] + on_x + on_z + on_y + on_l
+    partners = [on_core] + next_x + next_z + pair_y + pair_l
     barrier = pltpu.get_barrier_semaphore()
     for partner in partners:
         pl.semaphore_signal(barrier, inc=1, device_id=partner, device_id_type=MESH)
@@ -152,39 +166,59 @@
         for copy in copies:
             copy.wait_send()
 
-    stages = (on_z, on_x, [on_core], on_y, on_l)
-
-    def stat_copies(step):
-        return [
-            remote(
-                stat.at[step],
-                stat_in.at[step, d],
-                t_s.at[step, d],
-                t_r.at[step, d],
-                to,
-            )
-            for d, to in enumerate(stages[step])
-        ]
-
-    def stat_sum(step):
-        arrive(stat_copies(step))
-        total = stat[step]
-        for d in range(len(stages[step])):
-            total = total + stat_in[step, d]
-        stat[step + 1] = total
+    stages = [device(z=z) for z in pairs(mz, nz)]
+    stages += [device(x=x) for x in pairs(mx, nx)] + [on_core]
+    in_group = len(stages)
+    stages += pair_y + pair_l
+
+    def stat_copy(step):
+        return remote(
+            stat.at[step], stat_in.at[step], t_s.at[step], t_r.at[step], stages[step]
+        )
+
+    def stat_next(step):
+        if step < len(stages):
+            stat_copy(step).wait_recv()
+            stat[step + 1] = stat[step] + stat_in[step]
+            if step + 1 < len(stages):
+                stat_copy(step + 1).start()
 
     def gather_z():
         mine = kv.at[:, mc, mx, mz]
         return [
-            remote(mine, mine, gz_s.at[d], gz_r.at[d], to) for d, to in enumerate(on_z)
+            remote(mine, mine, gz_s.at[d], gz_r.at[d], to)
+            for d, to in enumerate(next_z)
+        ]
+
+    def relay_z():
+        if nz == 2:
+            return []
+        parts = [kv.at[0:2, mc, mx, near_z[1]], kv.at[2:4, mc, mx, near_z[0]]]
+        return [
+            remote(block, block, hz_s.at[d], hz_r.at[d], next_z[d])
+            for d, block in enumerate(parts)
         ]
 
     def gather_x(half):
         mine = kv.at[2 * half : 2 * half + 2, mc, mx]
         return [
             remote(mine, mine, gx_s.at[half, d], gx_r.at[half, d], to)
-            for d, to in enumerate(on_x)
-        ]
+            for d, to in enumerate(next_x)
+        ]
+
+    def relay_x(half):
+        if nx == 2:
+            return []
+        parts = [kv.at[2 * half, mc, near_x[1]], kv.at[2 * half + 1, mc, near_x[0]]]
+        return [
+            remote(block, block, hx_s.at[half, d], hx_r.at[half, d], next_x[d])
+            for d, block in enumerate(parts)
+        ]
+
+    def pass_on(copies, relays):
+        for d, copy in enumerate(copies):
+            copy.wait_recv()
+            start(relays[d : d + 1])
 
     def gather_c(half):
         mine = kv.at[2 * half : 2 * half + 2, mc]
@@ -221,13 +255,13 @@
             for d, to in enumerate(on_z)
         ]
 
-    def before_c(n):
-        cs[chunks[n]] = acc[chunks[n], 1 - mc].astype(BF16)
+    def before_c(n, advantage):
+        cs[chunks[n]] = (acc[chunks[n], 1 - mc] * advantage).astype(BF16)
         start(reduce_c(n))
 
-    def after_c(n):
+    def after_c(n, advantage):
         arrive(reduce_c(n))
-        both = acc[chunks[n], mc] + rc[chunks[n]].astype(F32)
+        both = acc[chunks[n], mc] * advantage + rc[chunks[n]].astype(F32)
         part[chunks[n]] = both
         xs[chunks[n]] = both.astype(BF16)
         start(reduce_x(n))
@@ -277,7 +311,7 @@
             up_v[:, cols] = (up_v[:, cols].astype(F32) * live).astype(BF16)
         dpo_ref[g] = dot(own_v[1, :, head_cols(g)], stacked(up_v, g), 1, 1)
 
-    def attend(g, advantage):
+    def attend(g):
         q_g, grad_out = stacked(q_v, g), stacked(up_v, g)
         s_ref[...] = dot(prompt_rows(g, 0), q_g, 1, 1)
         dp_ref[0:prompt] = dot(prompt_rows(g, 1), grad_out, 1, 1)
@@ -290,12 +324,12 @@
         e_ref[prompt:] = jnp.exp2((so_ref[g] - top) * (SCALE * LOG2E))
         inverse = 1.0 / jnp.sum(e_ref[...], axis=0, keepdims=True)
         pb_ref[...] = (e_ref[...] * inverse).astype(BF16)
-        grad_values = advantage * dot(pb_ref[...], grad_out, 1, 0)
+        grad_values = dot(pb_ref[...], grad_out, 1, 0)
         acc[g, :, :, :, 1] = grad_values[0:prompt].reshape(2, nx, nz, 16, HEAD)
         own_grad[1, :, head_cols(g)] = grad_values[prompt:]
         delta = jnp.sum(pb_ref[...].astype(F32) * dp_ref[...], axis=0, keepdims=True)
         ds_ref[g] = ((e_ref[...] * inverse) * (dp_ref[...] - delta)).astype(BF16)
-        grad_keys = (advantage * SCALE) * dot(ds_ref[g], q_g, 1, 0)
+        grad_keys = SCALE * dot(ds_ref[g], q_g, 1, 0)
         acc[g, :, :, :, 0] = grad_keys[0:prompt].reshape(2, nx, nz, 16, HEAD)
         own_grad[0, :, head_cols(g)] = grad_keys[prompt:]
 
@@ -314,54 +348,58 @@
         kv[g, mc, mx, mz, 1] = shard_v[1, :, head_cols(g)]
     pl.semaphore_wait(barrier, len(partners))
     start(gather_z())
-    start(stat_copies(0))
+    stat_copy(0).start()
+    pass_on(gather_z(), relay_z())
+    stat_next(0)
+    arrive(relay_z()[0:1])
+    start(gather_x(0))
+    arrive(relay_z()[1:2])
+    start(gather_x(1))
+    stat_next(1)
     for load in loads[2:]:
         load.wait()
     own_part(0)
+    pass_on(gather_x(0), relay_x(0))
+    stat_next(2)
     own_part(1)
-    arrive(gather_z())
-    start(gather_x(0))
-    start(gather_x(1))
-    stat_sum(0)
-    start(stat_copies(1))
+    pass_on(gather_x(1), relay_x(1))
+    arrive(relay_x(0))
+    start(gather_c(0))
+    stat_next(3)
     own_part(2)
+    arrive(relay_x(1))
+    start(gather_c(1))
     own_part(3)
-    arrive(gather_x(0))
-    start(gather_c(0))
-    stat_sum(1)
-    start(stat_copies(2))
-    arrive(gather_x(1))
-    start(gather_c(1))
-    stat_sum(2)
-    start(stat_copies(3))
-    advantage = reward - stat[3, 0:1] / (nz * nx * 2)
     arrive(gather_c(0))
-    attend(0, advantage)
-    attend(1, advantage)
-    before_c(0)
+    attend(0)
+    stat_next(4)
+    attend(1)
+    advantage = (reward - stat[in_group, 0:1] / (nz * nx * 2)).reshape(1, 1, 1, 1, 1, 128)
+    before_c(0, advantage)
     arrive(gather_c(1))
-    attend(2, advantage)
-    before_c(1)
-    after_c(0)
-    stat_sum(3)
-    start(stat_copies(4))
-    attend(3, advantage)
-    before_c(2)
-    after_c(1)
+    attend(2)
+    before_c(1, advantage)
+    after_c(0, advantage)
+    stat_next(5)
+    attend(3)
+    before_c(2, advantage)
+    after_c(1, advantage)
     after_x(0)
-    after_c(2)
-    stat_sum(4)
-    unit = 1.0 / stat[5, 8:9]
-    weight = advantage * SCALE * unit
-    query_gradient(0, weight)
+    stat_next(6)
+    after_c(2, advantage)
+    stat_next(7)
     after_x(1)
-    query_gradient(1, weight)
+    stat_next(8)
+    unit = 1.0 / stat[len(stages), 8:9]
+    weight = (reward - stat[in_group, 0:1] / (nz * nx * 2)) * unit
+    query_gradient(0, weight * SCALE)
+    query_gradient(1, weight * SCALE)
     after_x(2)
-    query_gradient(2, weight)
-    query_gradient(3, weight)
+    query_gradient(2, weight * SCALE)
+    query_gradient(3, weight * SCALE)
     for g in range(KEY_HEADS):
         for i in range(2):
-            go_v[i, :, head_cols(g)] = (own_grad[i, :, head_cols(g)] * unit).astype(BF16)
+            go_v[i, :, head_cols(g)] = (own_grad[i, :, head_cols(g)] * weight).astype(BF16)
     stores = [
         pltpu.make_async_copy(src, dst, out_sem.at[i])
         for i, (src, dst) in enumerate(
@@ -380,10 +418,12 @@
     after_z(2, unit)
     start(stores[3:5])
     for step in range(len(stages)):
-        drain(stat_copies(step))
+        stat_copy(step).wait_send()
     drain(gather_z())
+    drain(relay_z())
     for half in range(2):
         drain(gather_x(half))
+        drain(relay_x(half))
         drain(gather_c(half))
     for n in range(len(chunks)):
         drain(reduce_c(n))
@@ -428,7 +468,6 @@
     joined = prompt + TOKENS
     wide, narrow = queries.shape[3], response_keys.shape[3]
     shard = prompt_key_rows.shape[1]
-    most = max(dims) - 1
     vmem, sem = pltpu.VMEM, pltpu.SemaphoreType.DMA
     anywhere = pl.BlockSpec(memory_space=pl.ANY)
     scalar = pl.BlockSpec(memory_space=pltpu.SMEM)
@@ -453,8 +492,8 @@
             vmem((2, TOKENS, narrow), BF16),
             vmem((2, shard, narrow), BF16),
             vmem((kvh, 2, nx, nz, 2, 16, HEAD), BF16),
-            vmem((6, 16, 128), F32),
-            vmem((5, most, 16, 128), F32),
+            vmem((10, 16, 128), F32),
+            vmem((9, 16, 128), F32),
             vmem((2, TOKENS, narrow), F32),
             vmem((kvh, TOKENS, rows), F32),
             vmem((kvh, TOKENS, rows), F32),
@@ -473,10 +512,14 @@
             vmem((nz - 1, kvh, 2, 16, HEAD), BF16),
             sem((6,)),
             sem((5,)),
-            sem((nz - 1,)),
-            sem((nz - 1,)),
-            sem((2, nx - 1)),
-            sem((2, nx - 1)),
+            sem((2,)),
+            sem((2,)),
+            sem((2,)),
+            sem((2,)),
+            sem((2, 2)),
+            sem((2, 2)),
+            sem((2, 2)),
+            sem((2, 2)),
             sem((2,)),
             sem((2,)),
             sem((3,)),
@@ -485,8 +528,8 @@
             sem((3, nx - 1)),
             sem((3, nz - 1)),
             sem((3, nz - 1)),
-            sem((5, most)),
-            sem((5, most)),
+            sem((9,)),
+            sem((9,)),
         ],
         compiler_params=pltpu.CompilerParams(
             collective_id=0,

time: 61 us -> 63.7 us (1.044)
  the two profiles are of different devices: /device:TPU:1 before, /device:TPU:40 now
where the time goes in v4:
time: 63.7 us; the launch traced here: 63.5 us
  Pallas kernels  61.6 us (97%)
  between operations  1.93 us (3%)
    pallas_call x1, Pallas kernels, on_device(): pl.pallas_call(functools.partial(kernel, dims), out_shape=shapes, in_spec...  59.5 us
    pallas_call x1, Pallas kernels, on_device(): pl.pallas_call(store_kernel, out_shape=shapes, in_specs=[anywhere] * 5, o...  2.06 us

profile of v4, /device:TPU:40, one launch (start us, length us, event | category | flops | bytes accessed | tf_op | source)
XLA Modules:
  0.0 63.5 jit_solution(9001815508271603037)
XLA Ops:
  1.9 59.5 %shard_map.119 = (bf16[128,2048]{1,0:T(8,128)(2,1)}, bf16[128,512]{1,0:T(8,128)(2,1)}, bf16[128,512]{1,0:T(8,128)(2,1)}, f32[16,512]{1,0:T(8,128)}, f32[16,512]{1,0:T(8,128)}) custom-call(bf16[128,2048]{1,0:T(8,128)(2,1)} %bitcast.11, bf16[128,512]{1,0:T(8,128)(2,1)} %bitcast.14, bf16[128,512]{1,0:T(8,128)(2,1)} %bitcast.15, bf16[16,512]{1,0:T(8,128)(2,1)} %bitcast.20, ...), custom_call_target="tpu_custom_call" | custom-call | flops 1400000000 | bytes 3000000 | tf_op jit(solution)/shard_map/pallas_call | solution.py:481
  61.5 2.1 %shard_map.120 = (bf16[128,2048]{1,0:T(8,128)(2,1)}, bf16[128,512]{1,0:T(8,128)(2,1)}, bf16[128,512]{1,0:T(8,128)(2,1)}, f32[16,512]{1,0:T(8,128)}, f32[16,512]{1,0:T(8,128)}) custom-call(bf16[128,2048]{1,0:T(8,128)(2,1)} %get-tuple-element.15.refs_0_, bf16[128,512]{1,0:T(8,128)(2,1)} %get-tuple-element.16.refs_1_, ...), custom_call_target="tpu_custom_call" | custom-call | tf_op jit(solution)/shard_map/pallas_call | solution.py:552

commit v5 on v4

--- a/solution.py
+++ b/solution.py
@@ -70,12 +70,8 @@
     out_sem,
     gz_s,
     gz_r,
-    hz_s,
-    hz_r,
     gx_s,
     gx_r,
-    hx_s,
-    hx_r,
     gc_s,
     gc_r,
     sc_s,
@@ -113,22 +109,16 @@
             device_id_type=MESH,
         )
 
-    def ring(me, n):
-        return [lax.rem(me + 1, n)] + ([lax.rem(me + n - 1, n)] if n > 2 else [])
-
     def pairs(me, n):
         flip = [me + 1 - 2 * lax.rem(me, 2)] if n > 1 else []
         return flip + ([n - 1 - me] if n > 2 else [])
 
-    near_z, near_x = ring(mz, nz), ring(mx, nx)
     on_core = device(c=1 - mc)
-    next_z = [device(z=z) for z in near_z]
-    next_x = [device(x=x) for x in near_x]
     pair_y = [device(y=y) for y in pairs(my, ny)]
     pair_l = [device(l=l) for l in pairs(ml, nl)]
     on_x = [device(x=ahead(mx, d, nx)) for d in range(1, nx)]
     on_z = [device(z=ahead(mz, d, nz)) for d in range(1, nz)]
-    partners = [on_core] + next_x + next_z + pair_y + pair_l
+    partners = on_z + on_x + [on_core] + pair_y + pair_l
     barrier = pltpu.get_barrier_semaphore()
     for partner in partners:
         pl.semaphore_signal(barrier, inc=1, device_id=partner, device_id_type=MESH)
@@ -183,46 +173,33 @@
             if step + 1 < len(stages):
                 stat_copy(step + 1).start()
 
-    def gather_z():
-        mine = kv.at[:, mc, mx, mz]
+    pieces = (slice(0, 1), slice(1, 2), slice(2, 4))
+
+    def gather_z(n):
+        mine = kv.at[pieces[n], mc, mx, mz]
         return [
-            remote(mine, mine, gz_s.at[d], gz_r.at[d], to)
-            for d, to in enumerate(next_z)
+            remote(mine, mine, gz_s.at[n, d], gz_r.at[n, d], to)
+            for d, to in enumerate(on_z)
         ]
 
-    def relay_z():
-        if nz == 2:
-            return []
-        parts = [kv.at[0:2, mc, mx, near_z[1]], kv.at[2:4, mc, mx, near_z[0]]]
+    def gather_x(n):
+        mine = kv.at[pieces[n], mc, mx]
         return [
-            remote(block, block, hz_s.at[d], hz_r.at[d], next_z[d])
-            for d, block in enumerate(parts)
+            remote(mine, mine, gx_s.at[n, d], gx_r.at[n, d], to)
+            for d, to in enumerate(on_x)
         ]
 
-    def gather_x(half):
-        mine = kv.at[2 * half : 2 * half + 2, mc, mx]
-        return [
-            remote(mine, mine, gx_s.at[half, d], gx_r.at[half, d], to)
-            for d, to in enumerate(next_x)
-        ]
-
-    def relay_x(half):
-        if nx == 2:
-            return []
-        parts = [kv.at[2 * half, mc, near_x[1]], kv.at[2 * half + 1, mc, near_x[0]]]
-        return [
-            remote(block, block, hx_s.at[half, d], hx_r.at[half, d], next_x[d])
-            for d, block in enumerate(parts)
-        ]
-
-    def pass_on(copies, relays):
-        for d, copy in enumerate(copies):
-            copy.wait_recv()
-            start(relays[d : d + 1])
-
-    def gather_c(half):
-        mine = kv.at[2 * half : 2 * half + 2, mc]
-        return [remote(mine, mine, gc_s.at[half], gc_r.at[half], on_core)]
+    def gather_c(n):
+        mine = kv.at[pieces[n], mc]
+        return [remote(mine, mine, gc_s.at[n], gc_r.at[n], on_core)]
+
+    def z_to_x(n):
+        arrive(gather_z(n))
+        start(gather_x(n))
+
+    def x_to_c(n):
+        arrive(gather_x(n))
+        start(gather_c(n))
 
     chunks = (slice(0, 2), slice(2, 3), slice(3, 4))
 
@@ -347,47 +324,45 @@
         kv[g, mc, mx, mz, 0] = shard_v[0, :, head_cols(g)]
         kv[g, mc, mx, mz, 1] = shard_v[1, :, head_cols(g)]
     pl.semaphore_wait(barrier, len(partners))
-    start(gather_z())
+    start(gather_z(0))
+    start(gather_z(1))
+    start(gather_z(2))
     stat_copy(0).start()
-    pass_on(gather_z(), relay_z())
+    z_to_x(0)
     stat_next(0)
-    arrive(relay_z()[0:1])
-    start(gather_x(0))
-    arrive(relay_z()[1:2])
-    start(gather_x(1))
-    stat_next(1)
+    z_to_x(1)
     for load in loads[2:]:
         load.wait()
     own_part(0)
-    pass_on(gather_x(0), relay_x(0))
+    x_to_c(0)
+    z_to_x(2)
+    stat_next(1)
+    own_part(1)
+    x_to_c(1)
     stat_next(2)
-    own_part(1)
-    pass_on(gather_x(1), relay_x(1))
-    arrive(relay_x(0))
-    start(gather_c(0))
+    own_part(2)
     stat_next(3)
-    own_part(2)
-    arrive(relay_x(1))
-    start(gather_c(1))
-    own_part(3)
     arrive(gather_c(0))
     attend(0)
+    x_to_c(2)
     stat_next(4)
+    own_part(3)
+    arrive(gather_c(1))
     attend(1)
     advantage = (reward - stat[in_group, 0:1] / (nz * nx * 2)).reshape(1, 1, 1, 1, 1, 128)
     before_c(0, advantage)
-    arrive(gather_c(1))
+    stat_next(5)
+    arrive(gather_c(2))
     attend(2)
     before_c(1, advantage)
     after_c(0, advantage)
-    stat_next(5)
+    stat_next(6)
     attend(3)
     before_c(2, advantage)
     after_c(1, advantage)
     after_x(0)
-    stat_next(6)
+    stat_next(7)
     after_c(2, advantage)
-    stat_next(7)
     after_x(1)
     stat_next(8)
     unit = 1.0 / stat[len(stages), 8:9]
@@ -419,12 +394,10 @@
     start(stores[3:5])
     for step in range(len(stages)):
         stat_copy(step).wait_send()
-    drain(gather_z())
-    drain(relay_z())
-    for half in range(2):
-        drain(gather_x(half))
-        drain(relay_x(half))
-        drain(gather_c(half))
+    for n in range(len(pieces)):
+        drain(gather_z(n))
+        drain(gather_x(n))
+        drain(gather_c(n))
     for n in range(len(chunks)):
         drain(reduce_c(n))
         drain(reduce_x(n))
@@ -512,16 +485,12 @@
             vmem((nz - 1, kvh, 2, 16, HEAD), BF16),
             sem((6,)),
             sem((5,)),
-            sem((2,)),
-            sem((2,)),
-            sem((2,)),
-            sem((2,)),
-            sem((2, 2)),
-            sem((2, 2)),
-            sem((2, 2)),
-            sem((2, 2)),
-            sem((2,)),
-            sem((2,)),
+            sem((3, nz - 1)),
+            sem((3, nz - 1)),
+            sem((3, nx - 1)),
+            sem((3, nx - 1)),
+            sem((3,)),
+            sem((3,)),
             sem((3,)),
             sem((3,)),
             sem((3, nx - 1)),

time: 63.7 us -> 64.7 us (1.016)
  the two profiles are of different devices: /device:TPU:40 before, /device:TPU:1 now
where the time goes in v5:
time: 64.7 us; the launch traced here: 64 us
  Pallas kernels  62.1 us (96%)
  between operations  1.93 us (3%)
    pallas_call x1, Pallas kernels, on_device(): pl.pallas_call(functools.partial(kernel, dims), out_shape=shapes, in_spec...  60 us
    pallas_call x1, Pallas kernels, on_device(): pl.pallas_call(store_kernel, out_shape=shapes, in_specs=[anywhere] * 5, o...  2.06 us

profile of v5, /device:TPU:1, one launch (start us, length us, event | category | flops | bytes accessed | tf_op | source)
XLA Modules:
  0.0 64.0 jit_solution(8209059887731390299)
XLA Ops:
  1.9 60.0 %shard_map.119 = (bf16[128,2048]{1,0:T(8,128)(2,1)}, bf16[128,512]{1,0:T(8,128)(2,1)}, bf16[128,512]{1,0:T(8,128)(2,1)}, f32[16,512]{1,0:T(8,128)}, f32[16,512]{1,0:T(8,128)}) custom-call(bf16[128,2048]{1,0:T(8,128)(2,1)} %bitcast.11, bf16[128,512]{1,0:T(8,128)(2,1)} %bitcast.14, bf16[128,512]{1,0:T(8,128)(2,1)} %bitcast.15, bf16[16,512]{1,0:T(8,128)(2,1)} %bitcast.20, ...), custom_call_target="tpu_custom_call" | custom-call | flops 1400000000 | bytes 3000000 | tf_op jit(solution)/shard_map/pallas_call | solution.py:454
  61.9 2.1 %shard_map.120 = (bf16[128,2048]{1,0:T(8,128)(2,1)}, bf16[128,512]{1,0:T(8,128)(2,1)}, bf16[128,512]{1,0:T(8,128)(2,1)}, f32[16,512]{1,0:T(8,128)}, f32[16,512]{1,0:T(8,128)}) custom-call(bf16[128,2048]{1,0:T(8,128)(2,1)} %get-tuple-element.15.refs_0_, bf16[128,512]{1,0:T(8,128)(2,1)} %get-tuple-element.16.refs_1_, ...), custom_call_target="tpu_custom_call" | custom-call | tf_op jit(solution)/shard_map/pallas_call | solution.py:521

commit v6 on v5

--- a/solution.py
+++ b/solution.py
@@ -51,6 +51,7 @@
     stat,
     stat_in,
     own_grad,
+    inverse_ref,
     so_ref,
     dpo_ref,
     s_ref,
@@ -156,22 +157,30 @@
         for copy in copies:
             copy.wait_send()
 
-    stages = [device(z=z) for z in pairs(mz, nz)]
-    stages += [device(x=x) for x in pairs(mx, nx)] + [on_core]
-    in_group = len(stages)
-    stages += pair_y + pair_l
-
-    def stat_copy(step):
-        return remote(
-            stat.at[step], stat_in.at[step], t_s.at[step], t_r.at[step], stages[step]
-        )
+    stages = [on_z, on_x, [on_core]] + [[to] for to in pair_y + pair_l]
+    in_group = 3
+
+    def stat_copies(step):
+        return [
+            remote(
+                stat.at[step],
+                stat_in.at[step, d],
+                t_s.at[step, d],
+                t_r.at[step, d],
+                to,
+            )
+            for d, to in enumerate(stages[step])
+        ]
 
     def stat_next(step):
         if step < len(stages):
-            stat_copy(step).wait_recv()
-            stat[step + 1] = stat[step] + stat_in[step]
+            arrive(stat_copies(step))
+            total = stat[step]
+            for d in range(len(stages[step])):
+                total = total + stat_in[step, d]
+            stat[step + 1] = total
             if step + 1 < len(stages):
-                stat_copy(step + 1).start()
+                start(stat_copies(step + 1))
 
     pieces = (slice(0, 1), slice(1, 2), slice(2, 4))
 
@@ -288,7 +297,7 @@
             up_v[:, cols] = (up_v[:, cols].astype(F32) * live).astype(BF16)
         dpo_ref[g] = dot(own_v[1, :, head_cols(g)], stacked(up_v, g), 1, 1)
 
-    def attend(g):
+    def forward(g):
         q_g, grad_out = stacked(q_v, g), stacked(up_v, g)
         s_ref[...] = dot(prompt_rows(g, 0), q_g, 1, 1)
         dp_ref[0:prompt] = dot(prompt_rows(g, 1), grad_out, 1, 1)
@@ -301,6 +310,11 @@
         e_ref[prompt:] = jnp.exp2((so_ref[g] - top) * (SCALE * LOG2E))
         inverse = 1.0 / jnp.sum(e_ref[...], axis=0, keepdims=True)
         pb_ref[...] = (e_ref[...] * inverse).astype(BF16)
+        inverse_ref[...] = inverse
+
+    def backward(g):
+        q_g, grad_out = stacked(q_v, g), stacked(up_v, g)
+        inverse = inverse_ref[...]
         grad_values = dot(pb_ref[...], grad_out, 1, 0)
         acc[g, :, :, :, 1] = grad_values[0:prompt].reshape(2, nx, nz, 16, HEAD)
         own_grad[1, :, head_cols(g)] = grad_values[prompt:]
@@ -325,46 +339,48 @@
         kv[g, mc, mx, mz, 1] = shard_v[1, :, head_cols(g)]
     pl.semaphore_wait(barrier, len(partners))
     start(gather_z(0))
+    start(stat_copies(0))
     start(gather_z(1))
     start(gather_z(2))
-    stat_copy(0).start()
     z_to_x(0)
+    z_to_x(1)
     stat_next(0)
-    z_to_x(1)
     for load in loads[2:]:
         load.wait()
     own_part(0)
     x_to_c(0)
     z_to_x(2)
-    stat_next(1)
     own_part(1)
     x_to_c(1)
+    stat_next(1)
+    own_part(2)
+    arrive(gather_c(0))
+    forward(0)
+    x_to_c(2)
+    backward(0)
     stat_next(2)
-    own_part(2)
-    stat_next(3)
-    arrive(gather_c(0))
-    attend(0)
-    x_to_c(2)
-    stat_next(4)
     own_part(3)
     arrive(gather_c(1))
-    attend(1)
+    forward(1)
+    backward(1)
     advantage = (reward - stat[in_group, 0:1] / (nz * nx * 2)).reshape(1, 1, 1, 1, 1, 128)
     before_c(0, advantage)
-    stat_next(5)
+    stat_next(3)
     arrive(gather_c(2))
-    attend(2)
+    forward(2)
+    after_c(0, advantage)
+    backward(2)
     before_c(1, advantage)
-    after_c(0, advantage)
-    stat_next(6)
-    attend(3)
-    before_c(2, advantage)
+    stat_next(4)
+    forward(3)
     after_c(1, advantage)
     after_x(0)
-    stat_next(7)
+    backward(3)
+    before_c(2, advantage)
+    stat_next(5)
+    after_x(1)
     after_c(2, advantage)
-    after_x(1)
-    stat_next(8)
+    stat_next(6)
     unit = 1.0 / stat[len(stages), 8:9]
     weight = (reward - stat[in_group, 0:1] / (nz * nx * 2)) * unit
     query_gradient(0, weight * SCALE)
@@ -388,20 +404,22 @@
         )
     ]
     start(stores[0:3])
-    after_z(0, unit)
-    after_z(1, unit)
-    after_z(2, unit)
-    start(stores[3:5])
     for step in range(len(stages)):
-        stat_copy(step).wait_send()
+        drain(stat_copies(step))
     for n in range(len(pieces)):
         drain(gather_z(n))
         drain(gather_x(n))
         drain(gather_c(n))
+    after_z(0, unit)
+    after_z(1, unit)
     for n in range(len(chunks)):
         drain(reduce_c(n))
         drain(reduce_x(n))
-        drain(reduce_z(n))
+        if n + 1 < len(chunks):
+            drain(reduce_z(n))
+    after_z(2, unit)
+    start(stores[3:5])
+    drain(reduce_z(len(chunks) - 1))
     for store in stores:
         store.wait()
 
@@ -466,8 +484,9 @@
             vmem((2, shard, narrow), BF16),
             vmem((kvh, 2, nx, nz, 2, 16, HEAD), BF16),
             vmem((10, 16, 128), F32),
-            vmem((9, 16, 128), F32),
+            vmem((7, 3, 16, 128), F32),
             vmem((2, TOKENS, narrow), F32),
+            vmem((1, rows), F32),
             vmem((kvh, TOKENS, rows), F32),
             vmem((kvh, TOKENS, rows), F32),
             vmem((prompt, rows), F32),
@@ -497,8 +516,8 @@
             sem((3, nx - 1)),
             sem((3, nz - 1)),
             sem((3, nz - 1)),
-            sem((9,)),
-            sem((9,)),
+            sem((7, 3)),
+            sem((7, 3)),
         ],
         compiler_params=pltpu.CompilerParams(
             collective_id=0,

time: 64.7 us -> 62.6 us (0.968)
  Pallas kernels: 62.1 us -> 60.4 us
    pallas_call x1, Pallas kernels: 60 us -> 58.4 us  [on_device(): pl.pallas_call(functools.partial(kernel, dims), out_shape=shapes, in_spec...]
where the time goes in v6:
time: 62.6 us; the launch traced here: 62.3 us
  Pallas kernels  60.4 us (96%)
  between operations  1.93 us (3%)
    pallas_call x1, Pallas kernels, on_device(): pl.pallas_call(functools.partial(kernel, dims), out_shape=shapes, in_spec...  58.4 us
    pallas_call x1, Pallas kernels, on_device(): pl.pallas_call(store_kernel, out_shape=shapes, in_specs=[anywhere] * 5, o...  2.06 us

profile of v6, /device:TPU:1, one launch (start us, length us, event | category | flops | bytes accessed | tf_op | source)
XLA Modules:
  0.0 62.3 jit_solution(176968373245622640)
XLA Ops:
  1.9 58.4 %shard_map.119 = (bf16[128,2048]{1,0:T(8,128)(2,1)}, bf16[128,512]{1,0:T(8,128)(2,1)}, bf16[128,512]{1,0:T(8,128)(2,1)}, f32[16,512]{1,0:T(8,128)}, f32[16,512]{1,0:T(8,128)}) custom-call(bf16[128,2048]{1,0:T(8,128)(2,1)} %bitcast.11, bf16[128,512]{1,0:T(8,128)(2,1)} %bitcast.14, bf16[128,512]{1,0:T(8,128)(2,1)} %bitcast.15, bf16[16,512]{1,0:T(8,128)(2,1)} %bitcast.20, ...), custom_call_target="tpu_custom_call" | custom-call | flops 1400000000 | bytes 3000000 | tf_op jit(solution)/shard_map/pallas_call | solution.py:472
  60.3 2.1 %shard_map.120 = (bf16[128,2048]{1,0:T(8,128)(2,1)}, bf16[128,512]{1,0:T(8,128)(2,1)}, bf16[128,512]{1,0:T(8,128)(2,1)}, f32[16,512]{1,0:T(8,128)}, f32[16,512]{1,0:T(8,128)}) custom-call(bf16[128,2048]{1,0:T(8,128)(2,1)} %get-tuple-element.15.refs_0_, bf16[128,512]{1,0:T(8,128)(2,1)} %get-tuple-element.16.refs_1_, ...), custom_call_target="tpu_custom_call" | custom-call | tf_op jit(solution)/shard_map/pallas_call | solution.py:540

commit v7 on v6

--- a/solution.py
+++ b/solution.py
@@ -33,8 +33,8 @@
     pk_hbm,
     pv_hbm,
     up_hbm,
-    reward_ref,
-    length_ref,
+    reward_hbm,
+    length_hbm,
     gq_hbm,
     gok_hbm,
     gov_hbm,
@@ -52,6 +52,8 @@
     stat_in,
     own_grad,
     inverse_ref,
+    reward_ref,
+    length_ref,
     so_ref,
     dpo_ref,
     s_ref,
@@ -130,6 +132,8 @@
             (
                 (pk_hbm, shard_v.at[0]),
                 (pv_hbm, shard_v.at[1]),
+                (reward_hbm, reward_ref),
+                (length_hbm, length_ref),
                 (q_hbm, q_v),
                 (ok_hbm, own_v.at[0]),
                 (ov_hbm, own_v.at[1]),
@@ -140,6 +144,8 @@
     for load in loads:
         load.start()
 
+    loads[2].wait()
+    loads[3].wait()
     reward = reward_ref[0, 0]
     length = length_ref[0, 0]
     stat[0, 0:8] = jnp.full((8, 128), reward, F32)
@@ -182,13 +188,12 @@
             if step + 1 < len(stages):
                 start(stat_copies(step + 1))
 
-    pieces = (slice(0, 1), slice(1, 2), slice(2, 4))
-
-    def gather_z(n):
-        mine = kv.at[pieces[n], mc, mx, mz]
+    pieces = (slice(0, 2), slice(2, 4))
+
+    def gather_z():
+        mine = kv.at[:, mc, mx, mz]
         return [
-            remote(mine, mine, gz_s.at[n, d], gz_r.at[n, d], to)
-            for d, to in enumerate(on_z)
+            remote(mine, mine, gz_s.at[d], gz_r.at[d], to) for d, to in enumerate(on_z)
         ]
 
     def gather_x(n):
@@ -201,10 +206,6 @@
     def gather_c(n):
         mine = kv.at[pieces[n], mc]
         return [remote(mine, mine, gc_s.at[n], gc_r.at[n], on_core)]
-
-    def z_to_x(n):
-        arrive(gather_z(n))
-        start(gather_x(n))
 
     def x_to_c(n):
         arrive(gather_x(n))
@@ -271,11 +272,19 @@
             gp_v[1, :, head_cols(g)] = both[i, 1] * scale
 
     def head_cols(g):
-        return slice(g * HEAD, (g + 1) * HEAD)
+        if isinstance(g, int):
+            return slice(g * HEAD, (g + 1) * HEAD)
+        return pl.ds(pl.multiple_of(g * HEAD, HEAD), HEAD)
 
     def query_cols(g, j):
-        lower = (g * QUERY_PER_KV + j) * HEAD
-        return slice(lower, lower + HEAD)
+        return head_cols(g * QUERY_PER_KV + j)
+
+    def each(lower, upper, body):
+        def step(i, carry):
+            body(i)
+            return carry
+
+        lax.fori_loop(lower, upper, step, 0)
 
     def stacked(ref, g):
         return jnp.concatenate(
@@ -297,29 +306,60 @@
             up_v[:, cols] = (up_v[:, cols].astype(F32) * live).astype(BF16)
         dpo_ref[g] = dot(own_v[1, :, head_cols(g)], stacked(up_v, g), 1, 1)
 
+    def key_rows(i):
+        return pl.ds(pl.multiple_of(i * TOKENS, TOKENS), TOKENS)
+
+    tiles = prompt // TOKENS
+
+    def column(x):
+        return x.reshape(TOKENS // 8, 8, rows)
+
     def forward(g):
         q_g, grad_out = stacked(q_v, g), stacked(up_v, g)
-        s_ref[...] = dot(prompt_rows(g, 0), q_g, 1, 1)
+        s_ref[0:prompt] = dot(prompt_rows(g, 0), q_g, 1, 1)
+        s_ref[prompt:] = so_ref[g]
         dp_ref[0:prompt] = dot(prompt_rows(g, 1), grad_out, 1, 1)
         dp_ref[prompt:] = dpo_ref[g]
-        top = jnp.maximum(
-            jnp.max(s_ref[...], axis=0, keepdims=True),
-            jnp.max(so_ref[g], axis=0, keepdims=True),
-        )
-        e_ref[0:prompt] = jnp.exp2((s_ref[...] - top) * (SCALE * LOG2E))
-        e_ref[prompt:] = jnp.exp2((so_ref[g] - top) * (SCALE * LOG2E))
-        inverse = 1.0 / jnp.sum(e_ref[...], axis=0, keepdims=True)
-        pb_ref[...] = (e_ref[...] * inverse).astype(BF16)
-        inverse_ref[...] = inverse
+
+        def highest(i, top):
+            return jnp.maximum(top, jnp.max(column(s_ref[key_rows(i)]), axis=0))
+
+        top = lax.fori_loop(0, tiles + 1, highest, jnp.full((8, rows), -1e30, F32))
+        top = jnp.max(top, axis=0, keepdims=True)
+
+        def exponents(i, total):
+            e = jnp.exp2((s_ref[key_rows(i)] - top) * (SCALE * LOG2E))
+            e_ref[key_rows(i)] = e
+            return total + jnp.sum(column(e), axis=0)
+
+        total = lax.fori_loop(0, tiles + 1, exponents, jnp.zeros((8, rows), F32))
+        inverse_ref[...] = 1.0 / jnp.sum(total, axis=0, keepdims=True)
 
     def backward(g):
         q_g, grad_out = stacked(q_v, g), stacked(up_v, g)
         inverse = inverse_ref[...]
+
+        def narrow(i, delta):
+            probs = e_ref[key_rows(i)] * inverse
+            e_ref[key_rows(i)] = probs
+            probs_b = probs.astype(BF16)
+            pb_ref[key_rows(i)] = probs_b
+            return delta + jnp.sum(
+                column(probs_b.astype(F32) * dp_ref[key_rows(i)]), axis=0
+            )
+
+        delta = lax.fori_loop(0, tiles + 1, narrow, jnp.zeros((8, rows), F32))
+        delta = jnp.sum(delta, axis=0, keepdims=True)
+
+        def scores(i):
+            ds_ref[g, key_rows(i)] = (
+                e_ref[key_rows(i)] * (dp_ref[key_rows(i)] - delta)
+            ).astype(BF16)
+
+        each(0, tiles + 1, scores)
         grad_values = dot(pb_ref[...], grad_out, 1, 0)
         acc[g, :, :, :, 1] = grad_values[0:prompt].reshape(2, nx, nz, 16, HEAD)
         own_grad[1, :, head_cols(g)] = grad_values[prompt:]
-        delta = jnp.sum(pb_ref[...].astype(F32) * dp_ref[...], axis=0, keepdims=True)
-        ds_ref[g] = ((e_ref[...] * inverse) * (dp_ref[...] - delta)).astype(BF16)
         grad_keys = SCALE * dot(ds_ref[g], q_g, 1, 0)
         acc[g, :, :, :, 0] = grad_keys[0:prompt].reshape(2, nx, nz, 16, HEAD)
         own_grad[0, :, head_cols(g)] = grad_keys[prompt:]
@@ -338,35 +378,29 @@
         kv[g, mc, mx, mz, 0] = shard_v[0, :, head_cols(g)]
         kv[g, mc, mx, mz, 1] = shard_v[1, :, head_cols(g)]
     pl.semaphore_wait(barrier, len(partners))
-    start(gather_z(0))
+    start(gather_z())
     start(stat_copies(0))
-    start(gather_z(1))
-    start(gather_z(2))
-    z_to_x(0)
-    z_to_x(1)
+    for load in loads[4:]:
+        load.wait()
+    arrive(gather_z())
+    start(gather_x(0))
+    start(gather_x(1))
     stat_next(0)
-    for load in loads[2:]:
-        load.wait()
-    own_part(0)
+    each(0, 2, own_part)
     x_to_c(0)
-    z_to_x(2)
-    own_part(1)
     x_to_c(1)
     stat_next(1)
-    own_part(2)
+    each(2, 4, own_part)
     arrive(gather_c(0))
     forward(0)
-    x_to_c(2)
     backward(0)
     stat_next(2)
-    own_part(3)
-    arrive(gather_c(1))
     forward(1)
     backward(1)
     advantage = (reward - stat[in_group, 0:1] / (nz * nx * 2)).reshape(1, 1, 1, 1, 1, 128)
     before_c(0, advantage)
     stat_next(3)
-    arrive(gather_c(2))
+    arrive(gather_c(1))
     forward(2)
     after_c(0, advantage)
     backward(2)
@@ -383,11 +417,9 @@
     stat_next(6)
     unit = 1.0 / stat[len(stages), 8:9]
     weight = (reward - stat[in_group, 0:1] / (nz * nx * 2)) * unit
-    query_gradient(0, weight * SCALE)
-    query_gradient(1, weight * SCALE)
+    each(0, 2, lambda g: query_gradient(g, weight * SCALE))
     after_x(2)
-    query_gradient(2, weight * SCALE)
-    query_gradient(3, weight * SCALE)
+    each(2, 4, lambda g: query_gradient(g, weight * SCALE))
     for g in range(KEY_HEADS):
         for i in range(2):
             go_v[i, :, head_cols(g)] = (own_grad[i, :, head_cols(g)] * weight).astype(BF16)
@@ -406,8 +438,8 @@
     start(stores[0:3])
     for step in range(len(stages)):
         drain(stat_copies(step))
+    drain(gather_z())
     for n in range(len(pieces)):
-        drain(gather_z(n))
         drain(gather_x(n))
         drain(gather_c(n))
     after_z(0, unit)
@@ -461,7 +493,6 @@
     shard = prompt_key_rows.shape[1]
     vmem, sem = pltpu.VMEM, pltpu.SemaphoreType.DMA
     anywhere = pl.BlockSpec(memory_space=pl.ANY)
-    scalar = pl.BlockSpec(memory_space=pltpu.SMEM)
     shapes = (
         jax.ShapeDtypeStruct((TOKENS, wide), BF16),
         jax.ShapeDtypeStruct((TOKENS, narrow), BF16),
@@ -472,7 +503,7 @@
     results = pl.pallas_call(
         functools.partial(kernel, dims),
         out_shape=shapes,
-        in_specs=[anywhere] * 6 + [scalar] * 2,
+        in_specs=[anywhere] * 8,
         out_specs=[anywhere] * 5,
         scratch_shapes=[
             vmem((TOKENS, wide), BF16),
@@ -487,9 +518,11 @@
             vmem((7, 3, 16, 128), F32),
             vmem((2, TOKENS, narrow), F32),
             vmem((1, rows), F32),
+            pltpu.SMEM((1, 1), F32),
+            pltpu.SMEM((1, 1), jnp.int32),
             vmem((kvh, TOKENS, rows), F32),
             vmem((kvh, TOKENS, rows), F32),
-            vmem((prompt, rows), F32),
+            vmem((joined, rows), F32),
             vmem((joined, rows), F32),
             vmem((joined, rows), F32),
             vmem((joined, rows), BF16),
@@ -502,14 +535,14 @@
             vmem((nx - 1, kvh, nz, 2, 16, HEAD), BF16),
             vmem((kvh, nz, 2, 16, HEAD), BF16),
             vmem((nz - 1, kvh, 2, 16, HEAD), BF16),
-            sem((6,)),
+            sem((8,)),
             sem((5,)),
-            sem((3, nz - 1)),
-            sem((3, nz - 1)),
-            sem((3, nx - 1)),
-            sem((3, nx - 1)),
-            sem((3,)),
-            sem((3,)),
+            sem((nz - 1,)),
+            sem((nz - 1,)),
+            sem((2, nx - 1)),
+            sem((2, nx - 1)),
+            sem((2,)),
+            sem((2,)),
             sem((3,)),
             sem((3,)),
             sem((3, nx - 1)),

time: 62.6 us -> 64.5 us (1.030); the launches traced: 62.3 us -> 63.5 us
  Pallas kernels: 60.4 us -> 61.6 us
    pallas_call x1, Pallas kernels: 58.4 us -> 59.6 us  [on_device(): pl.pallas_call(functools.partial(kernel, dims), out_shape=shapes, in_spec...]
where the time goes in v7:
time: 64.5 us; the launch traced here: 63.5 us
  Pallas kernels  61.6 us (96%)
  between operations  1.93 us (3%)
    pallas_call x1, Pallas kernels, on_device(): pl.pallas_call(functools.partial(kernel, dims), out_shape=shapes, in_spec...  59.6 us
    pallas_call x1, Pallas kernels, on_device(): pl.pallas_call(store_kernel, out_shape=shapes, in_specs=[anywhere] * 5, o...  2.06 us

profile of v7, /device:TPU:1, one launch (start us, length us, event | category | flops | bytes accessed | tf_op | source)
XLA Modules:
  0.0 63.5 jit_solution(12363055090723124454)
XLA Ops:
  1.9 59.6 %shard_map.119 = (bf16[128,2048]{1,0:T(8,128)(2,1)}, bf16[128,512]{1,0:T(8,128)(2,1)}, bf16[128,512]{1,0:T(8,128)(2,1)}, f32[16,512]{1,0:T(8,128)}, f32[16,512]{1,0:T(8,128)}) custom-call(bf16[128,2048]{1,0:T(8,128)(2,1)} %bitcast.11, bf16[128,512]{1,0:T(8,128)(2,1)} %bitcast.14, bf16[128,512]{1,0:T(8,128)(2,1)} %bitcast.15, bf16[16,512]{1,0:T(8,128)(2,1)} %bitcast.20, ...), custom_call_target="tpu_custom_call" | custom-call | flops 1400000000 | bytes 3000000 | tf_op jit(solution)/shard_map/pallas_call | solution.py:503
  61.5 2.1 %shard_map.120 = (bf16[128,2048]{1,0:T(8,128)(2,1)}, bf16[128,512]{1,0:T(8,128)(2,1)}, bf16[128,512]{1,0:T(8,128)(2,1)}, f32[16,512]{1,0:T(8,128)}, f32[16,512]{1,0:T(8,128)}) custom-call(bf16[128,2048]{1,0:T(8,128)(2,1)} %get-tuple-element.15.refs_0_, bf16[128,512]{1,0:T(8,128)(2,1)} %get-tuple-element.16.refs_1_, ...), custom_call_target="tpu_custom_call" | custom-call | tf_op jit(solution)/shard_map/pallas_call | solution.py:573

commit v8 on v7

--- a/solution.py
+++ b/solution.py
@@ -13,7 +13,6 @@
 HEAD = 128
 TOKENS = 128
 SCALE = HEAD ** (-0.5)
-LOG2E = 1.4426950408889634
 F32 = jnp.float32
 BF16 = jnp.bfloat16
 VMEM_LIMIT = 56 * 1024 * 1024
@@ -112,16 +111,12 @@
             device_id_type=MESH,
         )
 
-    def pairs(me, n):
-        flip = [me + 1 - 2 * lax.rem(me, 2)] if n > 1 else []
-        return flip + ([n - 1 - me] if n > 2 else [])
-
     on_core = device(c=1 - mc)
-    pair_y = [device(y=y) for y in pairs(my, ny)]
-    pair_l = [device(l=l) for l in pairs(ml, nl)]
+    on_y = [device(y=ahead(my, d, ny)) for d in range(1, ny)]
+    on_l = [device(l=ahead(ml, d, nl)) for d in range(1, nl)]
     on_x = [device(x=ahead(mx, d, nx)) for d in range(1, nx)]
     on_z = [device(z=ahead(mz, d, nz)) for d in range(1, nz)]
-    partners = on_z + on_x + [on_core] + pair_y + pair_l
+    partners = on_z + on_x + [on_core] + on_y + on_l
     barrier = pltpu.get_barrier_semaphore()
     for partner in partners:
         pl.semaphore_signal(barrier, inc=1, device_id=partner, device_id_type=MESH)
@@ -163,7 +158,7 @@
         for copy in copies:
             copy.wait_send()
 
-    stages = [on_z, on_x, [on_core]] + [[to] for to in pair_y + pair_l]
+    stages = [on_z, on_x, [on_core], on_y, on_l]
     in_group = 3
 
     def stat_copies(step):
@@ -272,19 +267,11 @@
             gp_v[1, :, head_cols(g)] = both[i, 1] * scale
 
     def head_cols(g):
-        if isinstance(g, int):
-            return slice(g * HEAD, (g + 1) * HEAD)
-        return pl.ds(pl.multiple_of(g * HEAD, HEAD), HEAD)
+        return slice(g * HEAD, (g + 1) * HEAD)
 
     def query_cols(g, j):
-        return head_cols(g * QUERY_PER_KV + j)
-
-    def each(lower, upper, body):
-        def step(i, carry):
-            body(i)
-            return carry
-
-        lax.fori_loop(lower, upper, step, 0)
+        lower = (g * QUERY_PER_KV + j) * HEAD
+        return slice(lower, lower + HEAD)
 
     def stacked(ref, g):
         return jnp.concatenate(
@@ -306,60 +293,29 @@
             up_v[:, cols] = (up_v[:, cols].astype(F32) * live).astype(BF16)
         dpo_ref[g] = dot(own_v[1, :, head_cols(g)], stacked(up_v, g), 1, 1)
 
-    def key_rows(i):
-        return pl.ds(pl.multiple_of(i * TOKENS, TOKENS), TOKENS)
-
-    tiles = prompt // TOKENS
-
-    def column(x):
-        return x.reshape(TOKENS // 8, 8, rows)
-
     def forward(g):
         q_g, grad_out = stacked(q_v, g), stacked(up_v, g)
-        s_ref[0:prompt] = dot(prompt_rows(g, 0), q_g, 1, 1)
-        s_ref[prompt:] = so_ref[g]
+        s_ref[...] = dot(prompt_rows(g, 0), q_g, 1, 1)
         dp_ref[0:prompt] = dot(prompt_rows(g, 1), grad_out, 1, 1)
         dp_ref[prompt:] = dpo_ref[g]
-
-        def highest(i, top):
-            return jnp.maximum(top, jnp.max(column(s_ref[key_rows(i)]), axis=0))
-
-        top = lax.fori_loop(0, tiles + 1, highest, jnp.full((8, rows), -1e30, F32))
-        top = jnp.max(top, axis=0, keepdims=True)
-
-        def exponents(i, total):
-            e = jnp.exp2((s_ref[key_rows(i)] - top) * (SCALE * LOG2E))
-            e_ref[key_rows(i)] = e
-            return total + jnp.sum(column(e), axis=0)
-
-        total = lax.fori_loop(0, tiles + 1, exponents, jnp.zeros((8, rows), F32))
-        inverse_ref[...] = 1.0 / jnp.sum(total, axis=0, keepdims=True)
+        top = jnp.maximum(
+            jnp.max(s_ref[...], axis=0, keepdims=True),
+            jnp.max(so_ref[g], axis=0, keepdims=True),
+        )
+        e_ref[0:prompt] = jnp.exp((s_ref[...] - top) * SCALE)
+        e_ref[prompt:] = jnp.exp((so_ref[g] - top) * SCALE)
+        inverse = 1.0 / jnp.sum(e_ref[...], axis=0, keepdims=True)
+        pb_ref[...] = (e_ref[...] * inverse).astype(BF16)
+        inverse_ref[...] = inverse
 
     def backward(g):
         q_g, grad_out = stacked(q_v, g), stacked(up_v, g)
         inverse = inverse_ref[...]
-
-        def narrow(i, delta):
-            probs = e_ref[key_rows(i)] * inverse
-            e_ref[key_rows(i)] = probs
-            probs_b = probs.astype(BF16)
-            pb_ref[key_rows(i)] = probs_b
-            return delta + jnp.sum(
-                column(probs_b.astype(F32) * dp_ref[key_rows(i)]), axis=0
-            )
-
-        delta = lax.fori_loop(0, tiles + 1, narrow, jnp.zeros((8, rows), F32))
-        delta = jnp.sum(delta, axis=0, keepdims=True)
-
-        def scores(i):
-            ds_ref[g, key_rows(i)] = (
-                e_ref[key_rows(i)] * (dp_ref[key_rows(i)] - delta)
-            ).astype(BF16)
-
-        each(0, tiles + 1, scores)
         grad_values = dot(pb_ref[...], grad_out, 1, 0)
         acc[g, :, :, :, 1] = grad_values[0:prompt].reshape(2, nx, nz, 16, HEAD)
         own_grad[1, :, head_cols(g)] = grad_values[prompt:]
+        delta = jnp.sum(pb_ref[...].astype(F32) * dp_ref[...], axis=0, keepdims=True)
+        ds_ref[g] = ((e_ref[...] * inverse) * (dp_ref[...] - delta)).astype(BF16)
         grad_keys = SCALE * dot(ds_ref[g], q_g, 1, 0)
         acc[g, :, :, :, 0] = grad_keys[0:prompt].reshape(2, nx, nz, 16, HEAD)
         own_grad[0, :, head_cols(g)] = grad_keys[prompt:]
@@ -382,44 +338,46 @@
     start(stat_copies(0))
     for load in loads[4:]:
         load.wait()
+    own_part(0)
+    own_part(1)
     arrive(gather_z())
     start(gather_x(0))
     start(gather_x(1))
     stat_next(0)
-    each(0, 2, own_part)
+    own_part(2)
     x_to_c(0)
-    x_to_c(1)
+    own_part(3)
     stat_next(1)
-    each(2, 4, own_part)
     arrive(gather_c(0))
     forward(0)
+    x_to_c(1)
     backward(0)
     stat_next(2)
     forward(1)
     backward(1)
     advantage = (reward - stat[in_group, 0:1] / (nz * nx * 2)).reshape(1, 1, 1, 1, 1, 128)
     before_c(0, advantage)
-    stat_next(3)
     arrive(gather_c(1))
     forward(2)
+    stat_next(3)
     after_c(0, advantage)
     backward(2)
     before_c(1, advantage)
+    forward(3)
     stat_next(4)
-    forward(3)
     after_c(1, advantage)
     after_x(0)
     backward(3)
     before_c(2, advantage)
-    stat_next(5)
-    after_x(1)
-    after_c(2, advantage)
-    stat_next(6)
     unit = 1.0 / stat[len(stages), 8:9]
     weight = (reward - stat[in_group, 0:1] / (nz * nx * 2)) * unit
-    each(0, 2, lambda g: query_gradient(g, weight * SCALE))
+    query_gradient(0, weight * SCALE)
+    after_c(2, advantage)
+    after_x(1)
+    query_gradient(1, weight * SCALE)
+    query_gradient(2, weight * SCALE)
     after_x(2)
-    each(2, 4, lambda g: query_gradient(g, weight * SCALE))
+    query_gradient(3, weight * SCALE)
     for g in range(KEY_HEADS):
         for i in range(2):
             go_v[i, :, head_cols(g)] = (own_grad[i, :, head_cols(g)] * weight).astype(BF16)
@@ -515,14 +473,14 @@
             vmem((2, shard, narrow), BF16),
             vmem((kvh, 2, nx, nz, 2, 16, HEAD), BF16),
             vmem((10, 16, 128), F32),
-            vmem((7, 3, 16, 128), F32),
+            vmem((5, 3, 16, 128), F32),
             vmem((2, TOKENS, narrow), F32),
             vmem((1, rows), F32),
             pltpu.SMEM((1, 1), F32),
             pltpu.SMEM((1, 1), jnp.int32),
             vmem((kvh, TOKENS, rows), F32),
             vmem((kvh, TOKENS, rows), F32),
-            vmem((joined, rows), F32),
+            vmem((prompt, rows), F32),
             vmem((joined, rows), F32),
             vmem((joined, rows), F32),
             vmem((joined, rows), BF16),
@@ -549,8 +507,8 @@
             sem((3, nx - 1)),
             sem((3, nz - 1)),
             sem((3, nz - 1)),
-            sem((7, 3)),
-            sem((7, 3)),
+            sem((5, 3)),
+            sem((5, 3)),
         ],
         compiler_params=pltpu.CompilerParams(
             collective_id=0,

time: 64.5 us -> 63.1 us (0.978); the launches traced: 63.5 us -> 62.9 us
  no operation moved by 1% of the time
where the time goes in v8:
time: 63.1 us; the launch traced here: 62.9 us
  Pallas kernels  61 us (97%)
  between operations  1.93 us (3%)
    pallas_call x1, Pallas kernels, on_device(): pl.pallas_call(functools.partial(kernel, dims), out_shape=shapes, in_spec...  58.9 us
    pallas_call x1, Pallas kernels, on_device(): pl.pallas_call(store_kernel, out_shape=shapes, in_specs=[anywhere] * 5, o...  2.06 us

profile of v8, /device:TPU:1, one launch (start us, length us, event | category | flops | bytes accessed | tf_op | source)
XLA Modules:
  0.0 62.9 jit_solution(14936385808707336079)
XLA Ops:
  1.9 58.9 %shard_map.119 = (bf16[128,2048]{1,0:T(8,128)(2,1)}, bf16[128,512]{1,0:T(8,128)(2,1)}, bf16[128,512]{1,0:T(8,128)(2,1)}, f32[16,512]{1,0:T(8,128)}, f32[16,512]{1,0:T(8,128)}) custom-call(bf16[128,2048]{1,0:T(8,128)(2,1)} %bitcast.11, bf16[128,512]{1,0:T(8,128)(2,1)} %bitcast.14, bf16[128,512]{1,0:T(8,128)(2,1)} %bitcast.15, bf16[16,512]{1,0:T(8,128)(2,1)} %bitcast.20, ...), custom_call_target="tpu_custom_call" | custom-call | flops 1400000000 | bytes 3000000 | tf_op jit(solution)/shard_map/pallas_call | solution.py:461
  60.9 2.1 %shard_map.120 = (bf16[128,2048]{1,0:T(8,128)(2,1)}, bf16[128,512]{1,0:T(8,128)(2,1)}, bf16[128,512]{1,0:T(8,128)(2,1)}, f32[16,512]{1,0:T(8,128)}, f32[16,512]{1,0:T(8,128)}) custom-call(bf16[128,2048]{1,0:T(8,128)(2,1)} %get-tuple-element.15.refs_0_, bf16[128,512]{1,0:T(8,128)(2,1)} %get-tuple-element.16.refs_1_, ...), custom_call_target="tpu_custom_call" | custom-call | tf_op jit(solution)/shard_map/pallas_call | solution.py:531

commit v9 on v8

--- a/solution.py
+++ b/solution.py
@@ -32,8 +32,8 @@
     pk_hbm,
     pv_hbm,
     up_hbm,
-    reward_hbm,
-    length_hbm,
+    reward_ref,
+    length_ref,
     gq_hbm,
     gok_hbm,
     gov_hbm,
@@ -51,8 +51,6 @@
     stat_in,
     own_grad,
     inverse_ref,
-    reward_ref,
-    length_ref,
     so_ref,
     dpo_ref,
     s_ref,
@@ -127,8 +125,6 @@
             (
                 (pk_hbm, shard_v.at[0]),
                 (pv_hbm, shard_v.at[1]),
-                (reward_hbm, reward_ref),
-                (length_hbm, length_ref),
                 (q_hbm, q_v),
                 (ok_hbm, own_v.at[0]),
                 (ov_hbm, own_v.at[1]),
@@ -139,8 +135,6 @@
     for load in loads:
         load.start()
 
-    loads[2].wait()
-    loads[3].wait()
     reward = reward_ref[0, 0]
     length = length_ref[0, 0]
     stat[0, 0:8] = jnp.full((8, 128), reward, F32)
@@ -336,7 +330,7 @@
     pl.semaphore_wait(barrier, len(partners))
     start(gather_z())
     start(stat_copies(0))
-    for load in loads[4:]:
+    for load in loads[2:]:
         load.wait()
     own_part(0)
     own_part(1)
@@ -366,9 +360,9 @@
     forward(3)
     stat_next(4)
     after_c(1, advantage)
-    after_x(0)
     backward(3)
     before_c(2, advantage)
+    after_x(0)
     unit = 1.0 / stat[len(stages), 8:9]
     weight = (reward - stat[in_group, 0:1] / (nz * nx * 2)) * unit
     query_gradient(0, weight * SCALE)
@@ -451,6 +445,7 @@
     shard = prompt_key_rows.shape[1]
     vmem, sem = pltpu.VMEM, pltpu.SemaphoreType.DMA
     anywhere = pl.BlockSpec(memory_space=pl.ANY)
+    scalar = pl.BlockSpec(memory_space=pltpu.SMEM)
     shapes = (
         jax.ShapeDtypeStruct((TOKENS, wide), BF16),
         jax.ShapeDtypeStruct((TOKENS, narrow), BF16),
@@ -461,7 +456,7 @@
     results = pl.pallas_call(
         functools.partial(kernel, dims),
         out_shape=shapes,
-        in_specs=[anywhere] * 8,
+        in_specs=[anywhere] * 6 + [scalar] * 2,
         out_specs=[anywhere] * 5,
         scratch_shapes=[
             vmem((TOKENS, wide), BF16),
@@ -476,8 +471,6 @@
             vmem((5, 3, 16, 128), F32),
             vmem((2, TOKENS, narrow), F32),
             vmem((1, rows), F32),
-            pltpu.SMEM((1, 1), F32),
-            pltpu.SMEM((1, 1), jnp.int32),
             vmem((kvh, TOKENS, rows), F32),
             vmem((kvh, TOKENS, rows), F32),
             vmem((prompt, rows), F32),
@@ -493,7 +486,7 @@
             vmem((nx - 1, kvh, nz, 2, 16, HEAD), BF16),
             vmem((kvh, nz, 2, 16, HEAD), BF16),
             vmem((nz - 1, kvh, 2, 16, HEAD), BF16),
-            sem((8,)),
+            sem((6,)),
             sem((5,)),
             sem((nz - 1,)),
             sem((nz - 1,)),

time: 63.1 us -> 63 us (level)
  no operation moved by 1% of the time
where the time goes in v9:
time: 63 us; the launch traced here: 62.8 us
  Pallas kernels  60.9 us (97%)
  between operations  1.93 us (3%)
    pallas_call x1, Pallas kernels, on_device(): pl.pallas_call(functools.partial(kernel, dims), out_shape=shapes, in_spec...  58.8 us
    pallas_call x1, Pallas kernels, on_device(): pl.pallas_call(store_kernel, out_shape=shapes, in_specs=[anywhere] * 5, o...  2.06 us

profile of v9, /device:TPU:1, one launch (start us, length us, event | category | flops | bytes accessed | tf_op | source)
XLA Modules:
  0.0 62.8 jit_solution(8129836989760936948)
XLA Ops:
  1.9 58.8 %shard_map.119 = (bf16[128,2048]{1,0:T(8,128)(2,1)}, bf16[128,512]{1,0:T(8,128)(2,1)}, bf16[128,512]{1,0:T(8,128)(2,1)}, f32[16,512]{1,0:T(8,128)}, f32[16,512]{1,0:T(8,128)}) custom-call(bf16[128,2048]{1,0:T(8,128)(2,1)} %bitcast.11, bf16[128,512]{1,0:T(8,128)(2,1)} %bitcast.14, bf16[128,512]{1,0:T(8,128)(2,1)} %bitcast.15, bf16[16,512]{1,0:T(8,128)(2,1)} %bitcast.20, ...), custom_call_target="tpu_custom_call" | custom-call | flops 1400000000 | bytes 3000000 | tf_op jit(solution)/shard_map/pallas_call | solution.py:456
  60.7 2.1 %shard_map.120 = (bf16[128,2048]{1,0:T(8,128)(2,1)}, bf16[128,512]{1,0:T(8,128)(2,1)}, bf16[128,512]{1,0:T(8,128)(2,1)}, f32[16,512]{1,0:T(8,128)}, f32[16,512]{1,0:T(8,128)}) custom-call(bf16[128,2048]{1,0:T(8,128)(2,1)} %get-tuple-element.15.refs_0_, bf16[128,512]{1,0:T(8,128)(2,1)} %get-tuple-element.16.refs_1_, ...), custom_call_target="tpu_custom_call" | custom-call | tf_op jit(solution)/shard_map/pallas_call | solution.py:524

commit v10 on v3

--- a/solution.py
+++ b/solution.py
@@ -13,7 +13,6 @@
 HEAD = 128
 TOKENS = 128
 SCALE = HEAD ** (-0.5)
-LOG2E = 1.4426950408889634
 F32 = jnp.float32
 BF16 = jnp.bfloat16
 VMEM_LIMIT = 56 * 1024 * 1024
@@ -51,8 +50,6 @@
     stat,
     stat_in,
     own_grad,
-    so_ref,
-    dpo_ref,
     s_ref,
     e_ref,
     dp_ref,
@@ -269,32 +266,27 @@
         key = lax.broadcasted_iota(jnp.int32, (TOKENS, rows), 0)
         step = lax.broadcasted_iota(jnp.int32, (TOKENS, rows), 1) & (TOKENS - 1)
         scores = dot(own_v[0, :, head_cols(g)], stacked(q_v, g), 1, 1)
-        so_ref[g] = jnp.where(key <= step, scores, -1e30)
+        s_ref[g, prompt:] = jnp.where(key <= step, scores, -1e30)
         step = lax.broadcasted_iota(jnp.int32, (TOKENS, HEAD), 0)
         live = jnp.where(step < length, 1.0, 0.0)
         for j in range(QUERY_PER_KV):
             cols = query_cols(g, j)
             up_v[:, cols] = (up_v[:, cols].astype(F32) * live).astype(BF16)
-        dpo_ref[g] = dot(own_v[1, :, head_cols(g)], stacked(up_v, g), 1, 1)
+        dp_ref[g, prompt:] = dot(own_v[1, :, head_cols(g)], stacked(up_v, g), 1, 1)
 
     def attend(g, advantage):
         q_g, grad_out = stacked(q_v, g), stacked(up_v, g)
-        s_ref[...] = dot(prompt_rows(g, 0), q_g, 1, 1)
-        dp_ref[0:prompt] = dot(prompt_rows(g, 1), grad_out, 1, 1)
-        dp_ref[prompt:] = dpo_ref[g]
-        top = jnp.maximum(
-            jnp.max(s_ref[...], axis=0, keepdims=True),
-            jnp.max(so_ref[g], axis=0, keepdims=True),
-        )
-        e_ref[0:prompt] = jnp.exp2((s_ref[...] - top) * (SCALE * LOG2E))
-        e_ref[prompt:] = jnp.exp2((so_ref[g] - top) * (SCALE * LOG2E))
-        inverse = 1.0 / jnp.sum(e_ref[...], axis=0, keepdims=True)
-        pb_ref[...] = (e_ref[...] * inverse).astype(BF16)
-        grad_values = advantage * dot(pb_ref[...], grad_out, 1, 0)
+        s_ref[g, 0:prompt] = dot(prompt_rows(g, 0), q_g, 1, 1)
+        dp_ref[g, 0:prompt] = dot(prompt_rows(g, 1), grad_out, 1, 1)
+        top = jnp.max(s_ref[g], axis=0, keepdims=True)
+        e_ref[g] = jnp.exp((s_ref[g] - top) * SCALE)
+        inverse = 1.0 / jnp.sum(e_ref[g], axis=0, keepdims=True)
+        pb_ref[g] = (e_ref[g] * inverse).astype(BF16)
+        grad_values = advantage * dot(pb_ref[g], grad_out, 1, 0)
         acc[g, :, :, :, 1] = grad_values[0:prompt].reshape(2, nx, nz, 16, HEAD)
         own_grad[1, :, head_cols(g)] = grad_values[prompt:]
-        delta = jnp.sum(pb_ref[...].astype(F32) * dp_ref[...], axis=0, keepdims=True)
-        ds_ref[g] = ((e_ref[...] * inverse) * (dp_ref[...] - delta)).astype(BF16)
+        delta = jnp.sum(pb_ref[g].astype(F32) * dp_ref[g], axis=0, keepdims=True)
+        ds_ref[g] = ((e_ref[g] * inverse) * (dp_ref[g] - delta)).astype(BF16)
         grad_keys = (advantage * SCALE) * dot(ds_ref[g], q_g, 1, 0)
         acc[g, :, :, :, 0] = grad_keys[0:prompt].reshape(2, nx, nz, 16, HEAD)
         own_grad[0, :, head_cols(g)] = grad_keys[prompt:]
@@ -348,16 +340,16 @@
     attend(3, advantage)
     before_c(2)
     after_c(1)
-    after_x(0)
-    after_c(2)
     stat_sum(4)
     unit = 1.0 / stat[5, 8:9]
     weight = advantage * SCALE * unit
     query_gradient(0, weight)
+    after_c(2)
+    after_x(0)
+    query_gradient(1, weight)
     after_x(1)
-    query_gradient(1, weight)
+    query_gradient(2, weight)
     after_x(2)
-    query_gradient(2, weight)
     query_gradient(3, weight)
     for g in range(KEY_HEADS):
         for i in range(2):
@@ -375,20 +367,22 @@
         )
     ]
     start(stores[0:3])
-    after_z(0, unit)
-    after_z(1, unit)
-    after_z(2, unit)
-    start(stores[3:5])
     for step in range(len(stages)):
         drain(stat_copies(step))
     drain(gather_z())
     for half in range(2):
         drain(gather_x(half))
         drain(gather_c(half))
+    after_z(0, unit)
+    after_z(1, unit)
     for n in range(len(chunks)):
         drain(reduce_c(n))
         drain(reduce_x(n))
-        drain(reduce_z(n))
+        if n + 1 < len(chunks):
+            drain(reduce_z(n))
+    after_z(2, unit)
+    start(stores[3:5])
+    drain(reduce_z(len(chunks) - 1))
     for store in stores:
         store.wait()
 
@@ -456,12 +450,10 @@
             vmem((6, 16, 128), F32),
             vmem((5, most, 16, 128), F32),
             vmem((2, TOKENS, narrow), F32),
-            vmem((kvh, TOKENS, rows), F32),
-            vmem((kvh, TOKENS, rows), F32),
-            vmem((prompt, rows), F32),
-            vmem((joined, rows), F32),
-            vmem((joined, rows), F32),
-            vmem((joined, rows), BF16),
+            vmem((kvh, joined, rows), F32),
+            vmem((kvh, joined, rows), F32),
+            vmem((kvh, joined, rows), F32),
+            vmem((kvh, joined, rows), BF16),
             vmem((kvh, joined, rows), BF16),
             vmem((kvh, 2, nx, nz, 2, 16, HEAD), F32),
             vmem((kvh, nx, nz, 2, 16, HEAD), BF16),

time: 61 us -> 60.1 us (0.985)
  no operation moved by 1% of the time
where the time goes in v10:
time: 60.1 us; the launch traced here: 59.8 us
  Pallas kernels  57.9 us (96%)
  between operations  1.93 us (3%)
    pallas_call x1, Pallas kernels, on_device(): pl.pallas_call(functools.partial(kernel, dims), out_shape=shapes, in_spec...  55.9 us
    pallas_call x1, Pallas kernels, on_device(): pl.pallas_call(store_kernel, out_shape=shapes, in_specs=[anywhere] * 5, o...  2.06 us

profile of v10, /device:TPU:1, one launch (start us, length us, event | category | flops | bytes accessed | tf_op | source)
XLA Modules:
  0.0 59.8 jit_solution(13797376507244247700)
XLA Ops:
  1.9 55.9 %shard_map.119 = (bf16[128,2048]{1,0:T(8,128)(2,1)}, bf16[128,512]{1,0:T(8,128)(2,1)}, bf16[128,512]{1,0:T(8,128)(2,1)}, f32[16,512]{1,0:T(8,128)}, f32[16,512]{1,0:T(8,128)}) custom-call(bf16[128,2048]{1,0:T(8,128)(2,1)} %bitcast.11, bf16[128,512]{1,0:T(8,128)(2,1)} %bitcast.14, bf16[128,512]{1,0:T(8,128)(2,1)} %bitcast.15, bf16[16,512]{1,0:T(8,128)(2,1)} %bitcast.20, ...), custom_call_target="tpu_custom_call" | custom-call | flops 1400000000 | bytes 3000000 | tf_op jit(solution)/shard_map/pallas_call | solution.py:436
  57.8 2.1 %shard_map.120 = (bf16[128,2048]{1,0:T(8,128)(2,1)}, bf16[128,512]{1,0:T(8,128)(2,1)}, bf16[128,512]{1,0:T(8,128)(2,1)}, f32[16,512]{1,0:T(8,128)}, f32[16,512]{1,0:T(8,128)}) custom-call(bf16[128,2048]{1,0:T(8,128)(2,1)} %get-tuple-element.15.refs_0_, bf16[128,512]{1,0:T(8,128)(2,1)} %get-tuple-element.16.refs_1_, ...), custom_call_target="tpu_custom_call" | custom-call | tf_op jit(solution)/shard_map/pallas_call | solution.py:501

commit v11 on v10

--- a/solution.py
+++ b/solution.py
@@ -187,7 +187,7 @@
         mine = kv.at[2 * half : 2 * half + 2, mc]
         return [remote(mine, mine, gc_s.at[half], gc_r.at[half], on_core)]
 
-    chunks = (slice(0, 2), slice(2, 3), slice(3, 4))
+    chunks = (slice(0, 2), slice(2, 4))
 
     def reduce_c(n):
         return [
@@ -333,23 +333,20 @@
     before_c(0)
     arrive(gather_c(1))
     attend(2, advantage)
-    before_c(1)
     after_c(0)
     stat_sum(3)
     start(stat_copies(4))
     attend(3, advantage)
-    before_c(2)
-    after_c(1)
+    before_c(1)
     stat_sum(4)
     unit = 1.0 / stat[5, 8:9]
     weight = advantage * SCALE * unit
     query_gradient(0, weight)
-    after_c(2)
+    after_c(1)
     after_x(0)
     query_gradient(1, weight)
+    query_gradient(2, weight)
     after_x(1)
-    query_gradient(2, weight)
-    after_x(2)
     query_gradient(3, weight)
     for g in range(KEY_HEADS):
         for i in range(2):
@@ -374,13 +371,12 @@
         drain(gather_x(half))
         drain(gather_c(half))
     after_z(0, unit)
-    after_z(1, unit)
     for n in range(len(chunks)):
         drain(reduce_c(n))
         drain(reduce_x(n))
         if n + 1 < len(chunks):
             drain(reduce_z(n))
-    after_z(2, unit)
+    after_z(1, unit)
     start(stores[3:5])
     drain(reduce_z(len(chunks) - 1))
     for store in stores:
@@ -471,12 +467,12 @@
             sem((2, nx - 1)),
             sem((2,)),
             sem((2,)),
-            sem((3,)),
-            sem((3,)),
-            sem((3, nx - 1)),
-            sem((3, nx - 1)),
-            sem((3, nz - 1)),
-            sem((3, nz - 1)),
+            sem((2,)),
+            sem((2,)),
+            sem((2, nx - 1)),
+            sem((2, nx - 1)),
+            sem((2, nz - 1)),
+            sem((2, nz - 1)),
             sem((5, most)),
             sem((5, most)),
         ],

time: 60.1 us -> 60.9 us (1.013)
  no operation moved by 1% of the time
where the time goes in v11:
time: 60.9 us; the launch traced here: 60.2 us
  Pallas kernels  58.3 us (96%)
  between operations  1.93 us (3%)
    pallas_call x1, Pallas kernels, on_device(): pl.pallas_call(functools.partial(kernel, dims), out_shape=shapes, in_spec...  56.2 us
    pallas_call x1, Pallas kernels, on_device(): pl.pallas_call(store_kernel, out_shape=shapes, in_specs=[anywhere] * 5, o...  2.06 us

profile of v11, /device:TPU:1, one launch (start us, length us, event | category | flops | bytes accessed | tf_op | source)
XLA Modules:
  0.0 60.2 jit_solution(1886508365870728224)
XLA Ops:
  1.9 56.2 %shard_map.119 = (bf16[128,2048]{1,0:T(8,128)(2,1)}, bf16[128,512]{1,0:T(8,128)(2,1)}, bf16[128,512]{1,0:T(8,128)(2,1)}, f32[16,512]{1,0:T(8,128)}, f32[16,512]{1,0:T(8,128)}) custom-call(bf16[128,2048]{1,0:T(8,128)(2,1)} %bitcast.11, bf16[128,512]{1,0:T(8,128)(2,1)} %bitcast.14, bf16[128,512]{1,0:T(8,128)(2,1)} %bitcast.15, bf16[16,512]{1,0:T(8,128)(2,1)} %bitcast.20, ...), custom_call_target="tpu_custom_call" | custom-call | flops 1400000000 | bytes 3000000 | tf_op jit(solution)/shard_map/pallas_call | solution.py:432
  58.1 2.1 %shard_map.120 = (bf16[128,2048]{1,0:T(8,128)(2,1)}, bf16[128,512]{1,0:T(8,128)(2,1)}, bf16[128,512]{1,0:T(8,128)(2,1)}, f32[16,512]{1,0:T(8,128)}, f32[16,512]{1,0:T(8,128)}) custom-call(bf16[128,2048]{1,0:T(8,128)(2,1)} %get-tuple-element.15.refs_0_, bf16[128,512]{1,0:T(8,128)(2,1)} %get-tuple-element.16.refs_1_, ...), custom_call_target="tpu_custom_call" | custom-call | tf_op jit(solution)/shard_map/pallas_call | solution.py:497
